TPU v7x, 128 devices: a whole 4x4x4 slice. The times are simulated.
128 devices in a mesh: replica: 16 (over x_hi, z, core), shard: 8 (over x_lo, y).
Axes of the slice: x: 4 (x_hi: 2, x_lo: 2; x = x_hi * 2 + x_lo), y: 4, z: 4, core: 2. Of those that a mesh axis runs over, the one named last changes fastest.
Arguments:
- tokens: bfloat16 [16384, 896], P(('replica', 'shard')), may hold values from -6 to 6
- segments: int32 [16384], P(('replica', 'shard')), may hold values from 0 to 2, as said below
- attn_gain: bfloat16 [896], P('shard'), may hold values from 0.25 to 1.75
- w_query: bfloat16 [896, 896], P('shard'), may hold values from -0.1875 to 0.1875
- w_key: bfloat16 [896, 128], P('shard'), may hold values from -0.1875 to 0.1875
- w_value: bfloat16 [896, 128], P('shard'), may hold values from -0.1875 to 0.1875
- w_out: bfloat16 [896, 896], P('shard'), may hold values from -2 to 2
- ffn_gain: bfloat16 [896], P('shard'), may hold values from 0.25 to 1.75
- w_gate: bfloat16 [896, 4864], P('shard'), may hold values from -0.1875 to 0.1875
- w_up: bfloat16 [896, 4864], P('shard'), may hold values from -0.1875 to 0.1875
- w_down: bfloat16 [4864, 896], P('shard'), may hold values from -0.078125 to 0.078125
- cotangent: bfloat16 [16384, 896], P(('replica', 'shard')), may hold values from -6 to 6
Outputs:
- output: bfloat16 [16384, 896], P(('replica', 'shard'))
- grad_tokens: float32 [16384, 896], P(('replica', 'shard'))
- grad_attn_gain: float32 [896], P('shard')
- grad_query: float32 [896, 896], P('shard')
- grad_key: float32 [896, 128], P('shard')
- grad_value: float32 [896, 128], P('shard')
- grad_out: float32 [896, 896], P('shard')
- grad_ffn_gain: float32 [896], P('shard')
- grad_gate: float32 [896, 4864], P('shard')
- grad_up: float32 [896, 4864], P('shard')
- grad_down: float32 [4864, 896], P('shard')
Inputs may be any that keep to these rules, and one draw needn't show every extreme that they name: `segments`: in each sequence of 1024 tokens the segment numbers start at 0, never fall and take exactly the values 0, 1 and 2; segment 1 starts within the first 128 tokens of the sequence and ends within its last 128.
All inputs are finite; a program needn't handle non-finite values.
Results may differ from a plain program's by a relative error of at most 0.02.
Values may be sent and summed in bfloat16 or wider, within the bound.
A program may use at most 192 MiB of HBM per device.

v0:
```python
import jax
import jax.numpy as jnp
import numpy as np
from jax import lax
from jax.experimental import pallas as pl
from jax.experimental.pallas import tpu as pltpu
from jax.sharding import PartitionSpec as P

D = 896
H = 14
HD = 64
KVH = 2
GROUP = H // KVH
FF = 4864
FC = FF // 8
FH = FC // 2
ROWS = 128
LENGTH = 1024
WR = D // 8
EPS = 1e-05
THETA = 10000.0
SCALE = 0.125

F32 = jnp.float32
BF16 = jnp.bfloat16
MESH = pl.DeviceIdType.MESH


def coords():
    replica = lax.axis_index("replica")
    shard = lax.axis_index("shard")
    x = lax.div(replica, 8) * 2 + lax.div(shard, 4)
    return x, lax.rem(shard, 4), lax.rem(lax.div(replica, 2), 4), lax.rem(replica, 2)


def place(x, y, z, core):
    return (lax.div(x, 2) * 8 + z * 2 + core, lax.rem(x, 2) * 4 + y)


def wrap(value):
    return lax.rem(value + 8, 4)


def part_of(index, size, unit):
    return pl.ds(pl.multiple_of(index * size, unit), size)


def remote(src, dst, send, recv, device):
    return pltpu.make_async_remote_copy(
        src_ref=src, dst_ref=dst, send_sem=send, recv_sem=recv, device_id=device, device_id_type=MESH
    )


class Net:
    def __init__(self, ssem, rsem, peer):
        self.ssem, self.rsem, self.peer = ssem, rsem, peer
        self.ns = self.nr = 0
        self.open = []

    def sends(self, count):
        base = self.ns
        self.ns += count
        assert self.ns <= self.ssem.shape[0]
        return lambda index: self.ssem.at[base + index]

    def recvs(self, count):
        base = self.nr
        self.nr += count
        assert self.nr <= self.rsem.shape[0]
        return lambda index: self.rsem.at[base + index]

    def pair(self, count):
        return self.sends(count), self.recvs(count)

    def go(self, src, dst, send, recv, device, when=None):
        copy = remote(src, dst, send, recv, device)
        if when is None:
            copy.start()
        else:
            pl.when(when)(copy.start)
        self.open.append((copy, when))

    def landed(self, ref, recv, when=None):
        copy = remote(ref, ref, self.ssem.at[0], recv, self.peer)
        if when is None:
            copy.wait_recv()
        else:
            pl.when(when)(copy.wait_recv)

    def drain(self):
        done, self.open = self.open, []
        for copy, when in done:
            if when is None:
                copy.wait_send()
            else:
                pl.when(when)(copy.wait_send)


def signal(barrier, device):
    pl.semaphore_signal(barrier, inc=1, device_id=device, device_id_type=MESH)


def dot(left, right):
    return jnp.dot(left, right, preferred_element_type=F32)


def dot_nt(left, right):
    return lax.dot_general(left, right, (((1,), (1,)), ((), ())), preferred_element_type=F32)


SENDS = 256
RECVS = 256
LOCALS = 16


def layer_kernel(
    tokens, seg, gain_one, gain_two, freq,
    cot, wq, wk, wv, wo, wg, wu, wd,
    output, gtok, gain_o,
    attn_o, wide_o, d_o,
    misc, wqk, wvo, st, wgu, wdv, acts, da, kv, kc, vc, kt, vt, qs, mask, mixt, mid, gains, trig, lse,
    gua, own, pa, fr, via, dgate, dup, dwd,
    gmt, own_cot, dkv, rkv, gqk,
    rz, sz, rx, ru, su, ruz, sgu, agu, wide, rzd, sdz, rxd, agd, fin,
    xa, sa, rya, ryl, ta, rza, tile, rh, aout,
    gvec, gpack, gx, gsum, gy, gz, gh,
    ssem, rsem, lsem,
):
    x, y, z, c = coords()
    xl, xh = lax.rem(x, 2), lax.div(x, 2)
    s = xl * 4 + y
    t = 2 * y + c
    core_peer = place(x, y, z, 1 - c)
    net = Net(ssem, rsem, core_peer)

    def of_sequence(k):
        other = lax.rem(s + k, 8)
        return other, place(xh * 2 + lax.div(other, 4), lax.rem(other, 4), z, c)

    def along_z(k):
        return place(x, y, wrap(z + k), c)

    def along_x(k):
        return place(wrap(x + k), y, z, c)

    rows = part_of(s, WR, 16)
    own_rows = part_of(s, ROWS, 16)
    own_tokens = part_of(t, ROWS, 16)
    core_half = part_of(c, 512, 128)

    local = [
        pltpu.make_async_copy(wq.at[:, pl.ds(0, 384)], wqk.at[rows, pl.ds(0, 384)], lsem.at[2]),
        pltpu.make_async_copy(wk, wqk.at[rows, pl.ds(384, 128)], lsem.at[3]),
        pltpu.make_async_copy(wq.at[:, pl.ds(384, 512)], wqk.at[rows, pl.ds(512, 512)], lsem.at[4]),
        pltpu.make_async_copy(cot, acts.at[1, own_tokens], lsem.at[5]),
    ]
    own_index = 4 * c + z
    own_lanes = part_of(own_index, 128, 128)
    own_v = pltpu.make_async_copy(wv, wvo.at[rows, own_lanes], lsem.at[0])
    own_o = pltpu.make_async_copy(
        wo.at[:, part_of(own_index - jnp.where(own_index > 3, 1, 0), 128, 128)], wvo.at[rows, own_lanes], lsem.at[0]
    )
    pl.when(own_index == 3)(own_v.start)
    pl.when(own_index != 3)(own_o.start)
    for copy in local:
        copy.start()
    sender = xl == lax.div(z, 2)
    own_gate = pltpu.make_async_copy(wg, wide.at[0], lsem.at[6])
    own_up = pltpu.make_async_copy(wu, wide.at[0], lsem.at[6])
    pl.when(sender & (lax.rem(z, 2) == 0))(own_gate.start)
    pl.when(sender & (lax.rem(z, 2) == 1))(own_up.start)
    own_down = pltpu.make_async_copy(wd, wdv, lsem.at[7])
    pl.when(c == xl)(own_down.start)

    kv[...] = jnp.zeros_like(kv)
    rkv[...] = jnp.zeros_like(rkv)

    barrier = pltpu.get_barrier_semaphore()
    for k in range(1, 4):
        signal(barrier, place(x, wrap(y + k), z, c))
        signal(barrier, along_z(k))
    for d in (1, 3):
        for k in range(4):
            signal(barrier, place(wrap(x + d), wrap(y + k), z, c))
        signal(barrier, place(wrap(x + d), y, z, 1 - c))
    for k in range(4):
        signal(barrier, place(wrap(x + 2), wrap(y + k), z, c))
    signal(barrier, core_peer)
    misc[s] = jnp.zeros((8, 128), F32)
    misc[s, 0:1, 0:WR] = gain_one[...].astype(F32)
    misc[s, 1:2, 0:WR] = gain_two[...].astype(F32)
    misc[s, 2:3, :] = seg[...].astype(F32)

    pl.semaphore_wait(barrier, 21)

    ms, mr = net.pair(7)
    for k in range(1, 8):
        net.go(misc.at[s], misc.at[s], ms(k - 1), mr(k - 1), of_sequence(k)[1])

    pl.when(own_index == 3)(own_v.wait)
    pl.when(own_index != 3)(own_o.wait)
    os_, or_ = net.pair(7)
    for k in range(1, 8):
        part = wvo.at[rows, own_lanes]
        net.go(part, part, os_(k - 1), or_(k - 1), of_sequence(k)[1])

    for copy in local[0:3]:
        copy.wait()
    qs_s, qs_r = net.pair(11)
    for k in range(1, 4):
        part = wqk.at[rows, core_half]
        net.go(part, part, qs_s(k - 1), qs_r(k - 1), place(x, wrap(y + k), z, c))
    for k in range(4):
        for d in range(2):
            part = wqk.at[rows, part_of(2 * c + d, 256, 128)]
            i = 3 + 2 * k + d
            net.go(part, part, qs_s(i), qs_r(i), place(wrap(x + 1 - 2 * d), wrap(y + k), z, c))

    pl.when(sender & (lax.rem(z, 2) == 0))(own_gate.wait)
    pl.when(sender & (lax.rem(z, 2) == 1))(own_up.wait)

    @pl.when(sender)
    def _():
        for k in range(8):
            st[k] = wide[0, :, FC * k : FC * (k + 1)]

    matrix = lax.rem(z, 2)
    gs, gr = net.pair(8)
    for d in range(2):
        for k in range(4):
            if d == 0 and k == 0:
                continue
            target = place(xh * 2 + lax.rem(xl + d, 2), wrap(y + k), z, c)
            block = st.at[4 * c + wrap(y + k)]
            net.go(block, wgu.at[matrix, rows], gs(4 * d + k), gr(4 * d + k), target, when=sender)

    @pl.when(sender)
    def _():
        wgu[matrix, rows] = st[4 * c + y]

    for k in range(1, 8):
        net.landed(wvo.at[rows, own_lanes], or_(k - 1))
    oz_s, oz_r = net.pair(3)
    for k in range(1, 4):
        part = wvo.at[:, own_lanes]
        net.go(part, part, oz_s(k - 1), oz_r(k - 1), along_z(k))

    def block_rows(k):
        return part_of(4 * lax.div(z, 2) + wrap(y - k), WR, 16)

    gz_s, gz_r = net.pair(12)

    def block_along_z(k):
        part = wgu.at[matrix, block_rows(k)]
        for to in range(1, 4):
            net.go(part, part, gz_s(4 * to + k - 4), gz_r(4 * to + k - 4), along_z(to))

    net.landed(wgu.at[0, rows], gr(4), when=jnp.logical_not(sender))
    block_along_z(0)

    tok = tokens[...].astype(F32)
    unit = tok * lax.rsqrt(jnp.mean(tok * tok, axis=-1, keepdims=True) + EPS)

    for k in range(1, 8):
        net.landed(misc.at[0], mr(k - 1))
    for k in range(8):
        gains[0:8, WR * k : WR * (k + 1)] = misc[k, 0:8, 0:WR]
    numbers = misc[:, 2, :]
    zeros = jnp.sum(jnp.where(numbers < 0.5, 1.0, 0.0), keepdims=True)
    ones = jnp.sum(jnp.where((numbers > 0.5) & (numbers < 1.5), 1.0, 0.0), keepdims=True)
    own_numbers = misc[s, 2:3, :]
    begin = jnp.where(own_numbers < 0.5, 0.0, jnp.where(own_numbers < 1.5, zeros, zeros + ones))
    lane = lax.broadcasted_iota(jnp.int32, (1, ROWS), 1) + s * ROWS
    angle = freq[...] * (lane.astype(F32) - begin)
    trig[0] = jnp.cos(angle)
    trig[1] = jnp.sin(angle)
    key_place = lax.broadcasted_iota(jnp.int32, (LENGTH, ROWS), 0)
    allowed = (key_place >= begin.astype(jnp.int32)) & (key_place <= lane)
    mask[...] = jnp.where(allowed, 0.0, -1e30)
    normed = (unit * gains[0:1, :]).astype(BF16)
    normed_t = jnp.transpose(normed)

    qf_s, qf_r = net.pair(11)
    for i in range(11):
        if i < 3:
            part = wqk.at[part_of(xl * 4 + wrap(y - (i + 1)), WR, 16), core_half]
        else:
            k, d = divmod(i - 3, 2)
            part = wqk.at[part_of((1 - xl) * 4 + wrap(y - k), WR, 16), part_of(2 * c + d, 256, 128)]
        net.landed(part, qs_r(i))
        net.go(part, part, qf_s(i), qf_r(i), core_peer)
    for i in range(11):
        part = wqk.at[rows, pl.ds(0, 512 if i < 3 else 256)]
        net.landed(part, qf_r(i))
    raw = jnp.transpose(dot(normed, wqk[...]))
    cosine, sine = trig[0], trig[1]

    def rotated(head):
        at = HD * head + (128 if head > 5 else 0) if head < H else 384 + HD * (head - H)
        first = raw[at : at + 32]
        second = raw[at + 32 : at + 64]
        return first * cosine - second * sine, second * cosine + first * sine

    keys = jnp.concatenate([*rotated(H), *rotated(H + 1)], axis=0)
    kv[own_rows, 0:128] = jnp.transpose(keys).astype(BF16)

    ks, kr = net.pair(14)

    def to_later(which):
        part = kv.at[own_rows, pl.ds(128 * which, 128)]
        for k in range(1, 8):
            i = 7 * which + k - 1
            net.go(part, part, ks(i), kr(i), of_sequence(k)[1], when=s + k < 8)

    to_later(0)
    of_s, of_r = net.pair(4)
    for k in range(4):
        part = wvo.at[:, part_of(4 * c + wrap(z - k), 128, 128)]
        if k:
            net.landed(part, oz_r(k - 1))
        net.go(part, part, of_s(k), of_r(k), core_peer)
    for k in range(4):
        net.landed(wvo.at[:, own_lanes], of_r(k))

    kv[own_rows, 128:256] = dot(normed, wvo[:, 384:512]).astype(BF16)

    to_later(1)

    ds_, dr = net.sends(1), net.recvs(2)
    half = part_of(c, FH, 16)
    net.go(wd.at[half], wdv.at[half], ds_(0), dr(c), place(wrap(x + 1 - 2 * c), y, z, xl))

    def gather_tokens(which):
        ts, tr = net.pair(3)
        part = acts.at[which, own_tokens]
        for k in (1, 3, 2):
            net.go(part, part, ts(k - 1), tr(k - 1), place(x, wrap(y + k), z, c))
        return tr

    local[3].wait()
    cot_r = gather_tokens(1)

    for head in range(H):
        kv_head, j = divmod(head, GROUP)
        first, second = rotated(head)
        qs[kv_head, 0:32, ROWS * j : ROWS * (j + 1)] = (first * SCALE).astype(BF16)
        qs[kv_head, 32:64, ROWS * j : ROWS * (j + 1)] = (second * SCALE).astype(BF16)

    is_far = jnp.where(sender, 0, 1)
    for k in range(1, 4):
        net.landed(wgu.at[0, rows], gr(4 * is_far + k))
        block_along_z(k)

    for k in range(1, 8):
        for which in range(2):
            net.landed(kv.at[own_rows, pl.ds(0, 128)], kr(7 * which + k - 1), when=s - k >= 0)
    for head in range(KVH):
        keys = kv[:, HD * head : HD * (head + 1)]
        values = kv[:, 128 + HD * head : 128 + HD * (head + 1)]
        kc[head] = keys
        vc[head] = values
        kt[head] = jnp.transpose(keys)
        vt[head] = jnp.transpose(values)

    def attend(head, j, width):
        lanes = part_of(j, ROWS, 128) if width == 1 else pl.ds(pl.multiple_of(ROWS * j, 256), 2 * ROWS)
        raw_scores = dot(kc[head], qs[head, :, lanes])
        parts = []
        for i in range(width):
            scores = raw_scores[:, ROWS * i : ROWS * (i + 1)] + mask[...]
            highest = jnp.max(scores, axis=0, keepdims=True)
            weights = jnp.exp(scores - highest)
            total = jnp.sum(weights, axis=0, keepdims=True)
            parts.append((weights * (1.0 / total)).astype(BF16))
            lse[GROUP * head + j + i] = jnp.broadcast_to(highest + jnp.log(total), (8, ROWS))
        heads = dot(vt[head], jnp.concatenate(parts, axis=1) if width == 2 else parts[0])
        for i in range(width):
            mixt[part_of(GROUP * head + j + i, HD, HD)] = heads[:, ROWS * i : ROWS * (i + 1)]

    for p in range(GROUP // 2):
        for head in range(KVH):
            attend(head, 2 * p, 2)
    for head in range(KVH):
        attend(head, GROUP - 1, 1)

    attended_t = mixt[...].astype(BF16)
    attended = jnp.transpose(mixt[...]).astype(BF16)
    middle = tokens[...].astype(F32) + jnp.concatenate(
        [dot(attended, wvo[:, 0:384]), dot(attended, wvo[:, 512:1024])], axis=1
    )
    mid[...] = middle
    factor = lax.rsqrt(jnp.mean(middle * middle, axis=-1, keepdims=True) + EPS)
    acts[0, own_tokens] = (middle * factor * gains[1:2, :]).astype(BF16)

    n2_r = gather_tokens(0)

    def forward(which, off, send, recv):
        part = acts.at[which, part_of(2 * wrap(y - off) + c, ROWS, 16)]
        return remote(part, part, send(off), recv(off), core_peer)

    nf_s, nf_r = net.pair(4)
    cf_s, cf_r = net.pair(4)
    forward(0, 0, nf_s, nf_r).start()
    for off in (0, 1, 3, 2):
        if off:
            net.landed(acts.at[1, own_tokens], cot_r(off - 1))
        forward(1, off, cf_s, cf_r).start()
    pl.when(c == xl)(own_down.wait)
    for i in range(2):
        net.landed(wdv.at[pl.ds(FH * i, FH)], dr(i), when=c != xl)
    for i in range(12):
        net.landed(wgu.at[0, rows], gz_r(i))

    xsend, xrecv = net.pair(4)
    psend, precv = net.sends(8), net.recvs(6)
    vsend, vrecv = net.pair(2)

    def offset(k):
        return k

    def exchange(off):
        block = part_of(off, 256, 256)
        return remote(pa.at[0, block], pa.at[1, block], xsend(off), xrecv(off), core_peer)

    def part_copy(slot, core):
        off = (0, 1, 3)[slot]
        return remote(
            pa.at[0, pl.ds(256 * off + ROWS * core, ROWS)], fr.at[c, slot], psend(2 * slot + core),
            precv(3 * c + slot), place(x, wrap(y - off), z, core),
        )

    def through(side):
        rows_of = pl.ds(512 + ROWS * side, ROWS)
        return remote(pa.at[0, rows_of], via.at[side], vsend(side), vrecv(side), place(x, wrap(y - 1 + 2 * side), z, c))

    def add_cores(off):
        exchange(off).wait()
        block = pl.ds(256 * off, 256)
        total = own[off] + pa[1, block].astype(F32)
        if off % 2:
            side = off // 2
            through(side).wait_recv()
            half_of = slice(ROWS * side, ROWS * (side + 1))
            other = slice(ROWS * (1 - side), ROWS * (2 - side))
            pa[0, pl.ds(256 * off + ROWS * (1 - side), ROWS)] = total[other].astype(BF16)
            pa[0, pl.ds(256 * off + ROWS * side, ROWS)] = (total[half_of] + via[side].astype(F32)).astype(BF16)
        else:
            pa[0, block] = total.astype(BF16)

    def to_owners(off):
        add_cores(off)
        for core in range(2):
            if off == 2:
                through(core).start()
            elif off:
                part_copy(off - off // 3, core).start()
            else:

                @pl.when(c == core)
                def _():
                    fr[core, 0] = pa[0, ROWS * core : ROWS * (core + 1)]

                pl.when(c != core)(part_copy(0, core).start)

    @pl.loop(0, 4)
    def _(k):
        net.landed(acts.at[0, own_tokens], nf_r(offset(k)))
        net.landed(acts.at[1, own_tokens], cf_r(offset(k)))
        off = offset(k)
        block = part_of(wrap(y - off), 256, 256)
        normed_two = acts[0, block]
        cotangent = acts[1, block]
        gate = dot(normed_two, wgu[0])
        up = dot(normed_two, wgu[1])
        grad_hidden = dot_nt(cotangent, wdv[...])
        opening = 1.0 / (1.0 + jnp.exp(-gate))
        act = gate * opening
        hidden = (act * up).astype(BF16)
        grad_gate = (grad_hidden * up * opening * (1.0 + gate * (1.0 - opening))).astype(BF16)
        grad_up = (grad_hidden * act).astype(BF16)
        gua[0, block] = grad_gate
        gua[1, block] = grad_up
        da[1, 0:FC, block] = jnp.transpose(hidden)
        da[0, :, block] = jnp.transpose(normed_two)

        @pl.when(k < 3)
        def _():
            after = offset(k + 1)
            net.landed(acts.at[0, own_tokens], n2_r(after - 1))
            forward(0, after, nf_s, nf_r).start()

        pl.when(k == 1)(lambda: to_owners(0))
        pl.when(k == 3)(lambda: to_owners(2))

        out_part = dot(hidden, wdv[...])
        grad_part = dot_nt(grad_gate, wgu[0]) + dot_nt(grad_up, wgu[1])
        own[off] = jnp.where(c == 0, out_part, grad_part)
        pa[0, part_of(off, 256, 256)] = jnp.where(c == 0, grad_part, out_part).astype(BF16)
        exchange(off).start()

    for off in range(4):
        forward(0, off, nf_s, nf_r).wait_send()
        forward(1, off, cf_s, cf_r).wait_send()
    net.drain()

    def gradient(matrix_, store):
        for h in range(2):
            tall = dot(da[0, 448 * h : 448 * (h + 1)], gua[matrix_]).astype(BF16)
            for k in range(4):
                store[h, wrap(k - y)] = tall[WR * k : WR * (k + 1)]

    gradient(0, dgate)
    zs, zr = net.pair(3)
    for k in range(1, 4):
        net.go(dgate.at[:, wrap(z + k)], rz.at[k - 1], zs(k - 1), zr(k - 1), along_z(k))
    gradient(1, dup)
    us, ur = net.pair(3)
    for k in range(1, 4):
        part = dup.at[lax.rem(xl + k, 2), pl.ds(2 * lax.div(wrap(x + k), 2), 2)]
        net.go(part, ru.at[k - 1], us(k - 1), ur(k - 1), along_x(k))

    to_owners(1)
    to_owners(3)

    for h in range(2):
        tall = dot(da[1, FH * h : FH * (h + 1)], acts[1]).astype(BF16)
        for i in range(7):
            q = 7 * h + i
            dwd[q // 4, q % 4] = tall[:, 128 * i : 128 * (i + 1)]
    for q in (14, 15):
        dwd[q // 4, q % 4] = jnp.zeros((FH, 128), BF16)

    own_cot[...] = acts[1, own_tokens]

    @pl.loop(0, GROUP)
    def _(j):
        lanes = part_of(j, ROWS, 128)
        for head in range(KVH):
            scores = dot(kc[head], qs[head, :, lanes]) + mask[...]
            acts[head, :, lanes] = jnp.exp(scores - lse[GROUP * head + j, 0:1, :]).astype(BF16)

    for kind in range(2):
        for slot in range(3):
            net.landed(fr.at[kind, slot], precv(3 * kind + slot), when=None if slot else c != kind)
    middle = mid[...]
    total = fr[0, 0].astype(F32)
    grad_normed = fr[1, 0].astype(F32)
    for slot in range(1, 3):
        total = total + fr[0, slot].astype(F32)
        grad_normed = grad_normed + fr[1, slot].astype(F32)
    output[...] = (middle + total).astype(BF16)
    factor = lax.rsqrt(jnp.mean(middle * middle, axis=-1, keepdims=True) + EPS)
    unit_two = middle * factor
    scaled = grad_normed * gains[1:2, :]
    gvec[...] = jnp.broadcast_to(jnp.sum(grad_normed * unit_two, axis=0, keepdims=True), (8, D))
    grad_middle = own_cot[...].astype(F32) + factor * (
        scaled - unit_two * jnp.mean(scaled * unit_two, axis=-1, keepdims=True)
    )
    mid[...] = grad_middle

    branch = grad_middle.astype(BF16)
    grad_mixed = jnp.transpose(
        dot_nt(branch[:, 0:384], wvo[:, 0:384]) + dot_nt(branch[:, 384:D], wvo[:, 512:1024])
    )
    for head in range(H):
        kv_head, j = divmod(head, GROUP)
        gmt[kv_head, :, ROWS * j : ROWS * (j + 1)] = grad_mixed[HD * head : HD * (head + 1)].astype(BF16)
    grad_out = dot(attended_t, branch).astype(BF16)
    da[1, :, 0:384] = grad_out[:, 0:384]
    da[1, :, 512:1024] = grad_out[:, 384:D]
    first_of_peer = pl.ds(pl.multiple_of(512 * (1 - c), 128), 384)
    last_of_peer = pl.ds(pl.multiple_of(512 * (1 - c) + 384, 128), 128)
    first_own = pl.ds(pl.multiple_of(512 * c, 128), 384)
    last_own = pl.ds(pl.multiple_of(512 * c + 384, 128), 128)
    firsts, lasts_ = pl.ds(0, 384), pl.ds(384, 128)
    xas, xar = net.pair(5)
    net.go(da.at[1, :, first_of_peer], xa.at[1, :, firsts], xas(1), xar(1), core_peer)
    net.go(da.at[1, :, last_of_peer], xa.at[1, :, lasts_], xas(3), xar(3), core_peer, when=c == 0)

    for slot in range(3):
        for core in range(2):
            if slot:
                part_copy(slot, core).wait_send()
            else:
                pl.when(c != core)(part_copy(slot, core).wait_send)
    for side in range(2):
        through(side).wait_send()

    for k in range(1, 4):
        net.landed(ru.at[k - 1], ur(k - 1))
    for i in range(2):
        su[i] = (
            dup[xl, 2 * xh + i].astype(F32) + ru[0, i].astype(F32) + ru[1, i].astype(F32) + ru[2, i].astype(F32)
        ).astype(BF16)
    vs, vr = net.sends(2), net.recvs(4)
    for i in range(2):
        target = 2 * xh + i
        net.go(su.at[i], ruz.at[z], vs(i), vr(z), place(x, y, target, c), when=z != target)
    for k in range(1, 4):
        net.landed(rz.at[k - 1], zr(k - 1))
    for i in range(2):
        sz[i] = (
            dgate[i, z].astype(F32) + rz[0, i].astype(F32) + rz[1, i].astype(F32) + rz[2, i].astype(F32)
        ).astype(BF16)
    xs_s, xs_r = net.pair(3)
    for k in range(1, 4):
        net.go(sz.at[lax.rem(xl + k, 2)], rx.at[k - 1], xs_s(k - 1), xs_r(k - 1), along_x(k))

    def to_rows_owners(i, lanes, half_size, sems):
        for k in range(1, 4):
            other = part_of(xl * 4 + wrap(y + k), WR, 16)
            net.go(
                sa.at[i, other, lanes], rya.at[i, 0, k - 1, :, lanes], sems[0](k - 1), sems[1](k - 1),
                place(x, wrap(y + k), z, c),
            )
        for k in range(4):
            other = part_of((1 - xl) * 4 + wrap(y + k), WR, 16)
            for d, cut in enumerate(half_size):
                net.go(
                    sa.at[i, other, cut], rya.at[i, 1, k, :, cut], sems[0](3 + 2 * k + d), sems[1](3 + 2 * k + d),
                    place(wrap(x + 1 - 2 * d), wrap(y + k), z, c),
                )

    def from_rows_owners(i, lanes, half_size, sems):
        for k in range(1, 4):
            net.landed(rya.at[i, 0, k - 1, :, lanes], sems[1](k - 1))
        for k in range(4):
            for d, cut in enumerate(half_size):
                net.landed(rya.at[i, 1, k, :, cut], sems[1](3 + 2 * k + d))

    def last_tile(i, when):
        net.landed(xa.at[i, :, lasts_], xar(2 + i), when=when)

        @pl.when(when)
        def _():
            sa[i, :, 384:512] = (da[i, :, last_own].astype(F32) + xa[i, :, 384:512].astype(F32)).astype(BF16)

        for k in range(1, 8):
            other, target = of_sequence(k)
            part = sa.at[i, part_of(other, WR, 16), lasts_]
            net.go(part, ryl.at[i, k - 1], yl[i][0](k - 1), yl[i][1](k - 1), target, when=when)

    first_cuts = (pl.ds(0, 256), pl.ds(256, 128))
    yf = [net.pair(11), net.pair(11)]
    yl = [net.pair(7), net.pair(7)]
    net.landed(xa.at[1, :, firsts], xar(1))
    sa[1, :, 0:384] = (da[1, :, first_own].astype(F32) + xa[1, :, 0:384].astype(F32)).astype(BF16)
    to_rows_owners(1, firsts, first_cuts, yf[1])
    last_tile(1, c == 1)

    zds, zdr = net.pair(3)
    for k in range(1, 4):
        net.go(dwd.at[:, wrap(z + k)], rzd.at[k - 1], zds(k - 1), zdr(k - 1), along_z(k))

    def attend_back(head, j, width):
        lanes = part_of(j, ROWS, 128) if width == 1 else pl.ds(pl.multiple_of(ROWS * j, 256), 2 * ROWS)
        probs = acts[head, :, lanes].astype(F32)
        grad_probs = dot(vc[head], gmt[head, :, lanes])
        delta = jnp.sum(grad_probs * probs, axis=0, keepdims=True)
        grad_scores = (probs * (grad_probs - delta)).astype(BF16)
        pa[head, :, lanes] = grad_scores
        both = dot(kt[head], grad_scores) * SCALE
        cosine, sine = trig[0], trig[1]
        for i in range(width):
            rot = both[:, ROWS * i : ROWS * (i + 1)]
            at = HD * (GROUP * head + j + i)
            mixt[pl.ds(pl.multiple_of(at, 32), 32)] = rot[0:32] * cosine + rot[32:64] * sine
            mixt[pl.ds(pl.multiple_of(at + 32, 32), 32)] = rot[32:64] * cosine - rot[0:32] * sine

    kvs, kvr = net.pair(14)
    for head in range(KVH):
        for p in range(GROUP // 2):
            attend_back(head, 2 * p, 2)
        attend_back(head, GROUP - 1, 1)
        dkv[:, 128 * head : 128 * head + HD] = dot_nt(pa[head], qs[head]).astype(BF16)
        dkv[:, 128 * head + HD : 128 * (head + 1)] = dot_nt(acts[head], gmt[head]).astype(BF16)
        for k in range(1, 8):
            other, target = of_sequence(k)
            lanes = pl.ds(128 * head, 128)
            i = 7 * head + k - 1
            net.go(
                dkv.at[part_of(other, ROWS, 16), lanes], rkv.at[k - 1, :, lanes], kvs(i), kvr(i), target, when=s + k >= 8
            )

    grad_query = jnp.transpose(mixt[...]).astype(BF16)
    gqk[:, 0:384] = grad_query[:, 0:384]
    gqk[:, 512:1024] = grad_query[:, 384:D]
    part = dot(normed_t, grad_query).astype(BF16)
    da[0, :, 0:384] = part[:, 0:384]
    da[0, :, 512:1024] = part[:, 384:D]
    net.go(da.at[0, :, first_of_peer], xa.at[0, :, firsts], xas(0), xar(0), core_peer)
    net.go(da.at[0, :, last_of_peer], xa.at[0, :, lasts_], xas(2), xar(2), core_peer, when=c == 0)

    net.landed(xa.at[0, :, firsts], xar(0))
    sa[0, :, 0:384] = (da[0, :, first_own].astype(F32) + xa[0, :, 0:384].astype(F32)).astype(BF16)
    to_rows_owners(0, firsts, first_cuts, yf[0])
    last_tile(0, c == 1)

    for k in range(1, 4):
        net.landed(rx.at[k - 1], xs_r(k - 1))
    sgu[0] = (
        sz[xl].astype(F32) + rx[0].astype(F32) + rx[1].astype(F32) + rx[2].astype(F32)
    ).astype(BF16)
    own_block = 4 * c + y
    held = 4 * c + wrap(y - z)
    ags, agr = net.pair(4)
    net.go(sgu.at[0], agu.at[0, own_block], ags(0), agr(0), place(x, wrap(y + z), z, c), when=z != 0)

    @pl.when(z == 0)
    def _():
        agu[0, own_block] = sgu[0]

    cosine, sine = trig[0], trig[1]
    back, grad_values = [], []
    for head in range(KVH):
        lanes = slice(128 * head, 128 * (head + 1))
        total = dkv[own_rows, lanes].astype(F32)
        for k in range(1, 8):
            net.landed(rkv.at[k - 1, :, pl.ds(0, 128)], kvr(7 * head + k - 1), when=k > s)
            total = total + rkv[k - 1, :, lanes].astype(F32)
        keys = jnp.transpose(total)
        first, second = keys[0:32], keys[32:64]
        back += [first * cosine + second * sine, second * cosine - first * sine]
        grad_values.append(total[:, HD:128])
    grad_key = jnp.transpose(jnp.concatenate(back, axis=0)).astype(BF16)
    gqk[:, 384:512] = grad_key
    grad_value = jnp.concatenate(grad_values, axis=1).astype(BF16)
    da[0, :, 384:512] = dot(normed_t, grad_key).astype(BF16)
    da[1, :, 384:512] = dot(normed_t, grad_value).astype(BF16)
    for i in range(2):
        net.go(da.at[i, :, last_of_peer], xa.at[i, :, lasts_], xas(2 + i), xar(2 + i), core_peer, when=c == 1)

    for k in range(1, 4):
        net.landed(rzd.at[k - 1], zdr(k - 1))
    for i in range(4):
        sdz[i] = (
            dwd[i, z].astype(F32) + rzd[0, i].astype(F32) + rzd[1, i].astype(F32) + rzd[2, i].astype(F32)
        ).astype(BF16)
    xds, xdr = net.pair(3)
    for k in range(1, 4):
        net.go(sdz.at[wrap(x + k)], rxd.at[k - 1], xds(k - 1), xdr(k - 1), along_x(k))

    owner = xh == lax.div(z, 2)
    for k in range(4):
        net.landed(su.at[0], vr(k), when=owner & (z != k))
    ucs, ucr = net.pair(1)
    uhs = net.sends(1)

    @pl.when(owner)
    def _():
        ruz[z] = su[lax.rem(z, 2)]
        sgu[1] = (
            ruz[0].astype(F32) + ruz[1].astype(F32) + ruz[2].astype(F32) + ruz[3].astype(F32)
        ).astype(BF16)

    net.go(sgu.at[1], agu.at[1, own_block], ucs(0), ucr(0), place(x, wrap(y + z), z, c), when=owner & (z != 0))
    net.go(sgu.at[1], agu.at[1, own_block], uhs(0), ucr(0), place(wrap(x + 2), wrap(y + z), z, c), when=owner)

    @pl.when(owner & (z == 0))
    def _():
        agu[1, own_block] = sgu[1]

    grad_normed = dot_nt(gqk[...], wqk[...]) + dot_nt(grad_value, wvo[:, 384:512])
    tok = tokens[...].astype(F32)
    factor = lax.rsqrt(jnp.mean(tok * tok, axis=-1, keepdims=True) + EPS)
    unit = tok * factor
    scaled = grad_normed * gains[0:1, :]
    gtok[...] = mid[...] + factor * (scaled - unit * jnp.mean(scaled * unit, axis=-1, keepdims=True))
    gvec[0:1, :] = jnp.sum(grad_normed * unit, axis=0, keepdims=True)
    for row in range(2):
        for i in range(7):
            gpack[7 * row + i : 7 * row + i + 1, :] = gvec[row : row + 1, 128 * i : 128 * (i + 1)]
    net.go(gpack, gx, xas(4), xar(4), core_peer)

    for i in range(2):
        last_tile(i, c == 0)
    net.landed(gx, xar(4))
    gsum[...] = gpack[...] + gx[...]
    gys, gyr = net.pair(7)
    for k in range(1, 8):
        net.go(gsum, gy.at[k - 1], gys(k - 1), gyr(k - 1), of_sequence(k)[1])

    for k in range(1, 4):
        net.landed(rxd.at[k - 1], xdr(k - 1))
    agd[x, z] = (
        sdz[x].astype(F32) + rxd[0].astype(F32) + rxd[1].astype(F32) + rxd[2].astype(F32)
    ).astype(BF16)
    zas, zar = net.pair(3)
    for k in range(1, 4):
        net.go(agd.at[x, z], agd.at[x, z], zas(k - 1), zar(k - 1), along_z(k))

    afs, afr = net.pair(8)

    def spread(matrix_, sends, recvs):
        for k in range(1, 4):
            net.go(agu.at[matrix_, held], agu.at[matrix_, held], sends(k), recvs(k), along_z(k))
        net.go(agu.at[matrix_, held], agu.at[matrix_, held], afs(4 * matrix_), afr(4 * matrix_), core_peer)

    net.landed(agu.at[0, held], agr(0), when=z != 0)
    spread(0, ags, agr)

    zas2, zar2 = net.pair(6)
    for i in range(2):
        from_rows_owners(i, firsts, first_cuts, yf[i])
        total = sa[i, rows, 0:384].astype(F32)
        for k in range(3):
            total = total + rya[i, 0, k, :, 0:384].astype(F32)
        for k in range(4):
            total = total + rya[i, 1, k, :, 0:384].astype(F32)
        ta[i, :, 0:384] = total.astype(BF16)
        total = sa[i, rows, 384:512].astype(F32)
        for k in range(1, 8):
            net.landed(ryl.at[i, k - 1], yl[i][1](k - 1))
            total = total + ryl[i, k - 1].astype(F32)
        ta[i, :, 384:512] = total.astype(BF16)
    for k in range(1, 4):
        net.go(ta.at[:, :, part_of(wrap(z + k), 128, 128)], rza.at[k - 1], zas2(k - 1), zar2(k - 1), along_z(k))
    total = gsum[...]
    for k in range(1, 8):
        net.landed(gy.at[k - 1], gyr(k - 1))
        total = total + gy[k - 1]
    gz[3] = total
    for k in range(1, 4):
        net.go(gz.at[3], gz.at[k - 1], zas2(k + 2), zar2(k + 2), along_z(k))

    for k in range(1, 4):
        net.landed(agd.at[x, z], zar(k - 1))
    dxs, dxr = net.pair(3)
    for k in range(1, 4):
        net.go(agd.at[x], agd.at[x], dxs(k - 1), dxr(k - 1), along_x(k), when=lax.rem(xl + k, 2) == c)

    uas, uar = net.pair(4)
    net.landed(agu.at[1, held], ucr(0), when=jnp.logical_not(owner) | (z != 0))
    spread(1, uas, uar)

    for k in range(1, 4):
        net.landed(rza.at[k - 1], zar2(k - 1))
    tile[...] = (
        ta[:, :, part_of(z, 128, 128)].astype(F32)
        + rza[0].astype(F32) + rza[1].astype(F32) + rza[2].astype(F32)
    ).astype(BF16)
    total = gz[3]
    for k in range(1, 4):
        net.landed(gz.at[k - 1], zar2(k + 2))
        total = total + gz[k - 1]
    gh[1] = total
    hs, hr = net.pair(2)
    net.go(tile, rh, hs(0), hr(0), along_x(2))
    net.go(gh.at[1], gh.at[0], hs(1), hr(1), along_x(2))

    net.landed(rh, hr(0))
    own_tile = aout.at[:, :, own_lanes]
    aout[:, :, own_lanes] = (tile[...].astype(F32) + rh[...].astype(F32)).astype(BF16)
    lasts, lastr = net.pair(3)
    for k in range(1, 4):
        net.go(own_tile, own_tile, lasts(k - 1), lastr(k - 1), along_z(k))
    net.landed(gh.at[0], hr(1))
    gpack_sum = gh[0] + gh[1]
    gain_o[...] = jnp.zeros_like(gain_o)
    for row in range(2):
        for i in range(7):
            gain_o[row : row + 1, 128 * i : 128 * (i + 1)] = gpack_sum[7 * row + i : 7 * row + i + 1]

    outs = [
        pltpu.make_async_copy(aout, attn_o, lsem.at[9]),
        pltpu.make_async_copy(wide.at[0], wide_o.at[0], lsem.at[10]),
        pltpu.make_async_copy(wide.at[1], wide_o.at[1], lsem.at[11]),
    ]

    def to_other_core(matrix_, recvs):
        for k in (1, 3, 2):
            part = agu.at[matrix_, 4 * c + wrap(y - wrap(z - k))]
            net.landed(part, recvs(k))
            net.go(part, part, afs(4 * matrix_ + k), afr(4 * matrix_ + k), core_peer)

    def assemble(matrix_):
        for k in range(4):
            net.landed(agu.at[matrix_, held], afr(4 * matrix_ + k))
        for k in range(8):
            wide[matrix_, :, FC * k : FC * (k + 1)] = agu[matrix_, k]
        outs[1 + matrix_].start()

    to_other_core(0, agr)
    assemble(0)
    for k in range(1, 4):
        net.landed(agd.at[x], dxr(k - 1), when=xl == c)
    dfs, dfr = net.pair(1)
    net.go(agd, fin, dfs(0), dfr(0), core_peer, when=xl == c)
    own_sums = pltpu.make_async_copy(agd, d_o, lsem.at[8])
    pl.when(xl == c)(own_sums.start)
    for k in range(1, 4):
        net.landed(own_tile, lastr(k - 1))
    fs, fr_ = net.pair(1)
    part = aout.at[:, :, core_half]
    net.go(part, part, fs(0), fr_(0), core_peer)
    to_other_core(1, uar)
    net.landed(fin, dfr(0), when=xl != c)
    peer_sums = pltpu.make_async_copy(fin, d_o, lsem.at[8])
    pl.when(xl != c)(peer_sums.start)
    net.landed(aout.at[:, :, pl.ds(0, 512)], fr_(0))
    outs[0].start()
    assemble(1)

    net.drain()
    for copy in outs:
        copy.wait()
    pl.when(xl == c)(own_sums.wait)
    pl.when(xl != c)(peer_sums.wait)


def finish_kernel(
    out_in, tok_in, gain_in, attn_in, wide_in, down_in,
    one, two, out, tok, gq, gk, gv, go, gate, up, gdown,
    vout, vtok, gain, attn, wide, down, fq, fk, fv, fo, fgate, fup, fdown, isem, osem,
):
    ins = [
        pltpu.make_async_copy(source, target, isem.at[i])
        for i, (source, target) in enumerate(
            [(wide_in, wide), (down_in, down), (attn_in, attn), (tok_in, vtok), (out_in, vout), (gain_in, gain)]
        )
    ]
    for copy in ins:
        copy.start()
    outs = []

    def store(source, target):
        copy = pltpu.make_async_copy(source, target, osem.at[len(outs)])
        copy.start()
        outs.append(copy)

    ins[0].wait()
    fgate[...] = wide[0].astype(F32)
    store(fgate, gate)
    fup[...] = wide[1].astype(F32)
    store(fup, up)
    ins[1].wait()
    for q in range(14):
        h, i = divmod(q, 7)
        fdown[FH * h : FH * (h + 1), 128 * i : 128 * (i + 1)] = down[q // 4, q % 4].astype(F32)
    store(fdown, gdown)
    ins[2].wait()
    fq[:, 0:384] = attn[0, :, 0:384].astype(F32)
    fq[:, 384:D] = attn[0, :, 512:1024].astype(F32)
    store(fq, gq)
    fo[:, 0:384] = attn[1, :, 0:384].astype(F32)
    fo[:, 384:D] = attn[1, :, 512:1024].astype(F32)
    store(fo, go)
    fk[...] = attn[0, :, 384:512].astype(F32)
    store(fk, gk)
    fv[...] = attn[1, :, 384:512].astype(F32)
    store(fv, gv)
    ins[3].wait()
    store(vtok, tok)
    ins[4].wait()
    store(vout, out)
    ins[5].wait()
    shard = lax.axis_index("shard")
    for k in range(8):

        @pl.when(shard == k)
        def _():
            one[...] = gain[0:1, WR * k : WR * (k + 1)]
            two[...] = gain[1:2, WR * k : WR * (k + 1)]

    for copy in outs:
        copy.wait()


def vmem():
    return pl.BlockSpec(memory_space=pltpu.VMEM)


def anywhere():
    return pl.BlockSpec(memory_space=pl.ANY)


def shape(dims, dtype):
    return jax.ShapeDtypeStruct(dims, dtype)


def body(
    tokens, segments, attn_gain, w_query, w_key, w_value, w_out, ffn_gain, w_gate, w_up, w_down, cotangent
):
    half = HD // 2
    frequency = THETA ** (-(np.arange(half) * 2.0 / HD))
    freq = np.broadcast_to(frequency[:, None], (half, ROWS)).astype(np.float32)
    layer = pl.pallas_call(
        layer_kernel,
        name="layer",
        out_shape=[
            shape((ROWS, D), BF16),
            shape((ROWS, D), F32),
            shape((8, D), F32),
            shape((2, WR, 1024), BF16),
            shape((2, WR, FF), BF16),
            shape((4, 4, FH, 128), BF16),
        ],
        in_specs=[vmem()] * 5 + [anywhere()] * 8,
        out_specs=[vmem()] * 3 + [anywhere()] * 3,
        scratch_shapes=[
            pltpu.VMEM((8, 8, 128), F32),
            pltpu.VMEM((D, 1024), BF16),
            pltpu.VMEM((D, 1024), BF16),
            pltpu.VMEM((8, WR, FC), BF16),
            pltpu.VMEM((2, D, FC), BF16),
            pltpu.VMEM((FC, D), BF16),
            pltpu.VMEM((2, LENGTH, D), BF16),
            pltpu.VMEM((2, D, LENGTH), BF16),
            pltpu.VMEM((LENGTH, 256), BF16),
            pltpu.VMEM((KVH, LENGTH, HD), BF16),
            pltpu.VMEM((KVH, LENGTH, HD), BF16),
            pltpu.VMEM((KVH, HD, LENGTH), BF16),
            pltpu.VMEM((KVH, HD, LENGTH), BF16),
            pltpu.VMEM((KVH, HD, D), BF16),
            pltpu.VMEM((LENGTH, ROWS), F32),
            pltpu.VMEM((D, ROWS), F32),
            pltpu.VMEM((ROWS, D), F32),
            pltpu.VMEM((8, D), F32),
            pltpu.VMEM((2, half, ROWS), F32),
            pltpu.VMEM((H, 8, ROWS), F32),
            pltpu.VMEM((2, LENGTH, FC), BF16),
            pltpu.VMEM((4, 256, D), F32),
            pltpu.VMEM((2, LENGTH, D), BF16),
            pltpu.VMEM((2, 3, ROWS, D), BF16),
            pltpu.VMEM((2, ROWS, D), BF16),
            pltpu.VMEM((2, 4, WR, FC), BF16),
            pltpu.VMEM((2, 4, WR, FC), BF16),
            pltpu.VMEM((4, 4, FH, 128), BF16),
            pltpu.VMEM((KVH, HD, D), BF16),
            pltpu.VMEM((ROWS, D), BF16),
            pltpu.VMEM((LENGTH, 256), BF16),
            pltpu.VMEM((7, ROWS, 256), BF16),
            pltpu.VMEM((ROWS, 1024), BF16),
            pltpu.VMEM((3, 2, WR, FC), BF16),
            pltpu.VMEM((2, WR, FC), BF16),
            pltpu.VMEM((3, WR, FC), BF16),
            pltpu.VMEM((3, 2, WR, FC), BF16),
            pltpu.VMEM((2, WR, FC), BF16),
            pltpu.VMEM((4, WR, FC), BF16),
            pltpu.VMEM((2, WR, FC), BF16),
            pltpu.VMEM((2, 8, WR, FC), BF16),
            pltpu.VMEM((2, WR, FF), BF16),
            pltpu.VMEM((3, 4, FH, 128), BF16),
            pltpu.VMEM((4, FH, 128), BF16),
            pltpu.VMEM((3, FH, 128), BF16),
            pltpu.VMEM((4, 4, FH, 128), BF16),
            pltpu.VMEM((4, 4, FH, 128), BF16),
            pltpu.VMEM((2, D, 512), BF16),
            pltpu.VMEM((2, D, 512), BF16),
            pltpu.VMEM((2, 2, 4, WR, 384), BF16),
            pltpu.VMEM((2, 7, WR, 128), BF16),
            pltpu.VMEM((2, WR, 512), BF16),
            pltpu.VMEM((3, 2, WR, 128), BF16),
            pltpu.VMEM((2, WR, 128), BF16),
            pltpu.VMEM((2, WR, 128), BF16),
            pltpu.VMEM((2, WR, 1024), BF16),
            pltpu.VMEM((8, D), F32),
            pltpu.VMEM((16, 128), F32),
            pltpu.VMEM((16, 128), F32),
            pltpu.VMEM((16, 128), F32),
            pltpu.VMEM((7, 16, 128), F32),
            pltpu.VMEM((4, 16, 128), F32),
            pltpu.VMEM((2, 16, 128), F32),
            pltpu.SemaphoreType.DMA((SENDS,)),
            pltpu.SemaphoreType.DMA((RECVS,)),
            pltpu.SemaphoreType.DMA((LOCALS,)),
        ],
        compiler_params=pltpu.CompilerParams(
            collective_id=0, has_side_effects=True, vmem_limit_bytes=60 << 20
        ),
    )
    results = layer(
        tokens,
        segments.reshape(1, ROWS),
        attn_gain.reshape(1, WR),
        ffn_gain.reshape(1, WR),
        freq,
        cotangent,
        w_query,
        w_key,
        w_value,
        w_out,
        w_gate,
        w_up,
        w_down,
    )
    finish = pl.pallas_call(
        finish_kernel,
        name="finish",
        out_shape=[
            shape((1, WR), F32),
            shape((1, WR), F32),
            shape((ROWS, D), BF16),
            shape((ROWS, D), F32),
            shape((WR, D), F32),
            shape((WR, 128), F32),
            shape((WR, 128), F32),
            shape((WR, D), F32),
            shape((WR, FF), F32),
            shape((WR, FF), F32),
            shape((FC, D), F32),
        ],
        in_specs=[anywhere()] * 6,
        out_specs=[vmem()] * 2 + [anywhere()] * 9,
        scratch_shapes=[
            pltpu.VMEM((ROWS, D), BF16),
            pltpu.VMEM((ROWS, D), F32),
            pltpu.VMEM((8, D), F32),
            pltpu.VMEM((2, WR, 1024), BF16),
            pltpu.VMEM((2, WR, FF), BF16),
            pltpu.VMEM((4, 4, FH, 128), BF16),
            pltpu.VMEM((WR, D), F32),
            pltpu.VMEM((WR, 128), F32),
            pltpu.VMEM((WR, 128), F32),
            pltpu.VMEM((WR, D), F32),
            pltpu.VMEM((WR, FF), F32),
            pltpu.VMEM((WR, FF), F32),
            pltpu.VMEM((FC, D), F32),
            pltpu.SemaphoreType.DMA((6,)),
            pltpu.SemaphoreType.DMA((9,)),
        ],
        compiler_params=pltpu.CompilerParams(vmem_limit_bytes=62 << 20),
    )
    one, two, out, tok, gq, gk, gv, go, gate, up, down = finish(*results)
    return out, tok, one.reshape(WR), gq, gk, gv, go, two.reshape(WR), gate, up, down


def solution(mesh):
    tokens = P(("replica", "shard"), None)
    weight = P("shard", None)
    return jax.shard_map(
        body,
        mesh=mesh,
        in_specs=(
            tokens, P(("replica", "shard")), P("shard"), weight, weight, weight, weight,
            P("shard"), weight, weight, weight, tokens,
        ),
        out_specs=(
            tokens, tokens, P("shard"), weight, weight, weight, weight, P("shard"), weight, weight, weight,
        ),
        check_vma=False,
    )
```

profile of v0, /device:TPU:1, one launch (start us, length us, event | category | flops | bytes accessed | tf_op | source)
XLA Modules:
  0.0 158.4 jit_solution(16895392875762859521)
XLA Ops:
  0.6 152.0 %layer.1 = (bf16[128,896]{1,0:T(8,128)(2,1)}, f32[128,896]{1,0:T(8,128)}, f32[8,896]{1,0:T(8,128)}, bf16[2,112,1024]{2,1,0:T(8,128)(2,1)}, bf16[2,112,4864]{2,1,...) custom-call(bf16[128,896]{1,0:T(8,128)(2,1)} %tokens.1, s32[1,128]{1,0:T(1,128)} %bitcast.5, bf16[1,112]{1,0:T(2,128)(2,1)} %bitcast.6, ...), custom_call_target="tpu_custom_call" | custom-call | tf_op jit(solution)/shard_map/layer/pallas_call | solution.py:1072
  152.6 5.6 %finish.1 = (f32[1,112]{1,0:T(1,128)}, f32[1,112]{1,0:T(1,128)}, bf16[128,896]{1,0:T(8,128)(2,1)}, f32[128,896]{1,0:T(8,128)}, f32[112,896]{1,0:T(8,128)}, /*ind...) custom-call(bf16[128,896]{1,0:T(8,128)(2,1)} %get-tuple-element.28.o, ...), custom_call_target="tpu_custom_call" | custom-call | tf_op jit(solution)/shard_map/finish/pallas_call | solution.py:1124
where the time goes:
time: 159 us; the launch traced here: 158 us
  Pallas kernels  158 us (99%)
    pallas_call x1, Pallas kernels, body(): layer(tokens, segments.reshape(1, ROWS), attn_gain.reshape(1, WR), ffn_ga...  152 us
    pallas_call x1, Pallas kernels, body(): one, two, out, tok, gq, gk, gv, go, gate, up, down = finish(*results)  5.6 us

commit v1 on v0

--- a/solution.py
+++ b/solution.py
@@ -38,7 +38,7 @@
 
 
 def wrap(value):
-    return lax.rem(value + 8, 4)
+    return lax.rem(value + 16, 4)
 
 
 def part_of(index, size, unit):
@@ -108,22 +108,22 @@
     return lax.dot_general(left, right, (((1,), (1,)), ((), ())), preferred_element_type=F32)
 
 
-SENDS = 256
-RECVS = 256
+SENDS = 272
+RECVS = 272
 LOCALS = 16
 
 
 def layer_kernel(
     tokens, seg, gain_one, gain_two, freq,
     cot, wq, wk, wv, wo, wg, wu, wd,
-    output, gtok, gain_o,
-    attn_o, wide_o, d_o,
-    misc, wqk, wvo, st, wgu, wdv, acts, da, kv, kc, vc, kt, vt, qs, mask, mixt, mid, gains, trig, lse,
+    gain_o,
+    out_o, tok_o, attn_o, wide_o, d_o,
+    misc, wqk, wvo, wkv, st, wgu, wdv, acts, da, kv, kc, vc, kt, vt, qs, mask, mixt, mid, gains, trig, lse,
     gua, own, pa, fr, via, dgate, dup, dwd,
     gmt, own_cot, dkv, rkv, gqk,
     rz, sz, rx, ru, su, ruz, sgu, agu, wide, rzd, sdz, rxd, agd, fin,
     xa, sa, rya, ryl, ta, rza, tile, rh, aout,
-    gvec, gpack, gx, gsum, gy, gz, gh,
+    vout, vtok, gvec, gpack, gx, gsum, gy, gz, gh,
     ssem, rsem, lsem,
 ):
     x, y, z, c = coords()
@@ -148,11 +148,24 @@
     own_tokens = part_of(t, ROWS, 16)
     core_half = part_of(c, 512, 128)
 
+    barrier = pltpu.get_barrier_semaphore()
+    for k in range(1, 4):
+        signal(barrier, place(x, wrap(y + k), z, c))
+        signal(barrier, along_z(k))
+    for d in (1, 3):
+        for k in range(4):
+            signal(barrier, place(wrap(x + d), wrap(y + k), z, c))
+        signal(barrier, place(wrap(x + d), y, z, 1 - c))
+    for k in range(4):
+        signal(barrier, place(wrap(x + 2), wrap(y + k), z, c))
+    signal(barrier, core_peer)
     local = [
         pltpu.make_async_copy(wq.at[:, pl.ds(0, 384)], wqk.at[rows, pl.ds(0, 384)], lsem.at[2]),
         pltpu.make_async_copy(wk, wqk.at[rows, pl.ds(384, 128)], lsem.at[3]),
         pltpu.make_async_copy(wq.at[:, pl.ds(384, 512)], wqk.at[rows, pl.ds(512, 512)], lsem.at[4]),
         pltpu.make_async_copy(cot, acts.at[1, own_tokens], lsem.at[5]),
+        pltpu.make_async_copy(wk, wkv.at[0, rows], lsem.at[12]),
+        pltpu.make_async_copy(wv, wkv.at[1, rows], lsem.at[13]),
     ]
     own_index = 4 * c + z
     own_lanes = part_of(own_index, 128, 128)
@@ -172,20 +185,6 @@
     own_down = pltpu.make_async_copy(wd, wdv, lsem.at[7])
     pl.when(c == xl)(own_down.start)
 
-    kv[...] = jnp.zeros_like(kv)
-    rkv[...] = jnp.zeros_like(rkv)
-
-    barrier = pltpu.get_barrier_semaphore()
-    for k in range(1, 4):
-        signal(barrier, place(x, wrap(y + k), z, c))
-        signal(barrier, along_z(k))
-    for d in (1, 3):
-        for k in range(4):
-            signal(barrier, place(wrap(x + d), wrap(y + k), z, c))
-        signal(barrier, place(wrap(x + d), y, z, 1 - c))
-    for k in range(4):
-        signal(barrier, place(wrap(x + 2), wrap(y + k), z, c))
-    signal(barrier, core_peer)
     misc[s] = jnp.zeros((8, 128), F32)
     misc[s, 0:1, 0:WR] = gain_one[...].astype(F32)
     misc[s, 1:2, 0:WR] = gain_two[...].astype(F32)
@@ -196,6 +195,12 @@
     ms, mr = net.pair(7)
     for k in range(1, 8):
         net.go(misc.at[s], misc.at[s], ms(k - 1), mr(k - 1), of_sequence(k)[1])
+
+    for copy in local[4:6]:
+        copy.wait()
+    es, er = net.pair(7)
+    for k in range(1, 8):
+        net.go(wkv.at[c, rows], wkv.at[c, rows], es(k - 1), er(k - 1), of_sequence(k)[1])
 
     pl.when(own_index == 3)(own_v.wait)
     pl.when(own_index != 3)(own_o.wait)
@@ -203,6 +208,30 @@
     for k in range(1, 8):
         part = wvo.at[rows, own_lanes]
         net.go(part, part, os_(k - 1), or_(k - 1), of_sequence(k)[1])
+
+    pl.when(sender & (lax.rem(z, 2) == 0))(own_gate.wait)
+    pl.when(sender & (lax.rem(z, 2) == 1))(own_up.wait)
+
+    for core in range(2):
+
+        @pl.when(sender & (c == core))
+        def _():
+            for k in range(4):
+                st[k] = wide[0, :, FC * (4 * core + k) : FC * (4 * core + k + 1)]
+
+    matrix = lax.rem(z, 2)
+    gs, gr = net.pair(8)
+    for d in range(2):
+        for k in range(4):
+            if d == 0 and k == 0:
+                continue
+            target = place(xh * 2 + lax.rem(xl + d, 2), wrap(y + k), z, c)
+            block = st.at[wrap(y + k)]
+            net.go(block, wgu.at[matrix, rows], gs(4 * d + k), gr(4 * d + k), target, when=sender)
+
+    @pl.when(sender)
+    def _():
+        wgu[matrix, rows] = st[y]
 
     for copy in local[0:3]:
         copy.wait()
@@ -216,34 +245,15 @@
             i = 3 + 2 * k + d
             net.go(part, part, qs_s(i), qs_r(i), place(wrap(x + 1 - 2 * d), wrap(y + k), z, c))
 
-    pl.when(sender & (lax.rem(z, 2) == 0))(own_gate.wait)
-    pl.when(sender & (lax.rem(z, 2) == 1))(own_up.wait)
-
-    @pl.when(sender)
-    def _():
-        for k in range(8):
-            st[k] = wide[0, :, FC * k : FC * (k + 1)]
-
-    matrix = lax.rem(z, 2)
-    gs, gr = net.pair(8)
-    for d in range(2):
-        for k in range(4):
-            if d == 0 and k == 0:
-                continue
-            target = place(xh * 2 + lax.rem(xl + d, 2), wrap(y + k), z, c)
-            block = st.at[4 * c + wrap(y + k)]
-            net.go(block, wgu.at[matrix, rows], gs(4 * d + k), gr(4 * d + k), target, when=sender)
-
-    @pl.when(sender)
-    def _():
-        wgu[matrix, rows] = st[4 * c + y]
-
     for k in range(1, 8):
-        net.landed(wvo.at[rows, own_lanes], or_(k - 1))
-    oz_s, oz_r = net.pair(3)
-    for k in range(1, 4):
-        part = wvo.at[:, own_lanes]
-        net.go(part, part, oz_s(k - 1), oz_r(k - 1), along_z(k))
+
+        @pl.when(s + k < 8)
+        def _():
+            kv[part_of(s + k, ROWS, 16)] = jnp.zeros((ROWS, 256), BF16)
+
+        @pl.when(k <= s)
+        def _():
+            rkv[k - 1] = jnp.zeros((ROWS, 256), BF16)
 
     def block_rows(k):
         return part_of(4 * lax.div(z, 2) + wrap(y - k), WR, 16)
@@ -257,6 +267,13 @@
 
     net.landed(wgu.at[0, rows], gr(4), when=jnp.logical_not(sender))
     block_along_z(0)
+
+    for k in range(1, 8):
+        net.landed(wvo.at[rows, own_lanes], or_(k - 1))
+    oz_s, oz_r = net.pair(3)
+    for k in range(1, 4):
+        part = wvo.at[:, own_lanes]
+        net.go(part, part, oz_s(k - 1), oz_r(k - 1), along_z(k))
 
     tok = tokens[...].astype(F32)
     unit = tok * lax.rsqrt(jnp.mean(tok * tok, axis=-1, keepdims=True) + EPS)
@@ -280,6 +297,48 @@
     normed = (unit * gains[0:1, :]).astype(BF16)
     normed_t = jnp.transpose(normed)
 
+    ef_s, ef_r = net.pair(7)
+    for k in range(1, 8):
+        part = wkv.at[c, part_of(lax.rem(s + 8 - k, 8), WR, 16)]
+        net.landed(part, er(k - 1))
+        net.go(part, part, ef_s(k - 1), ef_r(k - 1), core_peer)
+    for k in range(1, 8):
+        net.landed(wkv.at[c, rows], ef_r(k - 1))
+    cosine, sine = trig[0], trig[1]
+
+    def rotated(raw, at):
+        first = raw[at : at + 32]
+        second = raw[at + 32 : at + 64]
+        return first * cosine - second * sine, second * cosine + first * sine
+
+    raw_keys = jnp.transpose(dot(normed, wkv[0]))
+    keys = jnp.concatenate([*rotated(raw_keys, 0), *rotated(raw_keys, HD)], axis=0)
+    kv[own_rows, 0:128] = jnp.transpose(keys).astype(BF16)
+    kv[own_rows, 128:256] = dot(normed, wkv[1]).astype(BF16)
+
+    ks, kr = net.pair(7)
+    for k in range(1, 8):
+        net.go(kv.at[own_rows], kv.at[own_rows], ks(k - 1), kr(k - 1), of_sequence(k)[1], when=s + k < 8)
+
+    is_far = jnp.where(sender, 0, 1)
+    for k in range(1, 4):
+        net.landed(wgu.at[0, rows], gr(4 * is_far + k))
+        block_along_z(k)
+
+    ds_, dr = net.sends(1), net.recvs(2)
+    half = part_of(c, FH, 16)
+    net.go(wd.at[half], wdv.at[half], ds_(0), dr(c), place(wrap(x + 1 - 2 * c), y, z, xl))
+
+    def gather_tokens(which):
+        ts, tr = net.pair(3)
+        part = acts.at[which, own_tokens]
+        for k in (1, 3, 2):
+            net.go(part, part, ts(k - 1), tr(k - 1), place(x, wrap(y + k), z, c))
+        return tr
+
+    local[3].wait()
+    cot_r = gather_tokens(1)
+
     qf_s, qf_r = net.pair(11)
     for i in range(11):
         if i < 3:
@@ -289,71 +348,18 @@
             part = wqk.at[part_of((1 - xl) * 4 + wrap(y - k), WR, 16), part_of(2 * c + d, 256, 128)]
         net.landed(part, qs_r(i))
         net.go(part, part, qf_s(i), qf_r(i), core_peer)
+
     for i in range(11):
-        part = wqk.at[rows, pl.ds(0, 512 if i < 3 else 256)]
-        net.landed(part, qf_r(i))
+        net.landed(wqk.at[rows, pl.ds(0, 512 if i < 3 else 256)], qf_r(i))
     raw = jnp.transpose(dot(normed, wqk[...]))
-    cosine, sine = trig[0], trig[1]
-
-    def rotated(head):
-        at = HD * head + (128 if head > 5 else 0) if head < H else 384 + HD * (head - H)
-        first = raw[at : at + 32]
-        second = raw[at + 32 : at + 64]
-        return first * cosine - second * sine, second * cosine + first * sine
-
-    keys = jnp.concatenate([*rotated(H), *rotated(H + 1)], axis=0)
-    kv[own_rows, 0:128] = jnp.transpose(keys).astype(BF16)
-
-    ks, kr = net.pair(14)
-
-    def to_later(which):
-        part = kv.at[own_rows, pl.ds(128 * which, 128)]
-        for k in range(1, 8):
-            i = 7 * which + k - 1
-            net.go(part, part, ks(i), kr(i), of_sequence(k)[1], when=s + k < 8)
-
-    to_later(0)
-    of_s, of_r = net.pair(4)
-    for k in range(4):
-        part = wvo.at[:, part_of(4 * c + wrap(z - k), 128, 128)]
-        if k:
-            net.landed(part, oz_r(k - 1))
-        net.go(part, part, of_s(k), of_r(k), core_peer)
-    for k in range(4):
-        net.landed(wvo.at[:, own_lanes], of_r(k))
-
-    kv[own_rows, 128:256] = dot(normed, wvo[:, 384:512]).astype(BF16)
-
-    to_later(1)
-
-    ds_, dr = net.sends(1), net.recvs(2)
-    half = part_of(c, FH, 16)
-    net.go(wd.at[half], wdv.at[half], ds_(0), dr(c), place(wrap(x + 1 - 2 * c), y, z, xl))
-
-    def gather_tokens(which):
-        ts, tr = net.pair(3)
-        part = acts.at[which, own_tokens]
-        for k in (1, 3, 2):
-            net.go(part, part, ts(k - 1), tr(k - 1), place(x, wrap(y + k), z, c))
-        return tr
-
-    local[3].wait()
-    cot_r = gather_tokens(1)
-
     for head in range(H):
         kv_head, j = divmod(head, GROUP)
-        first, second = rotated(head)
+        first, second = rotated(raw, HD * head + (128 if head > 5 else 0))
         qs[kv_head, 0:32, ROWS * j : ROWS * (j + 1)] = (first * SCALE).astype(BF16)
         qs[kv_head, 32:64, ROWS * j : ROWS * (j + 1)] = (second * SCALE).astype(BF16)
 
-    is_far = jnp.where(sender, 0, 1)
-    for k in range(1, 4):
-        net.landed(wgu.at[0, rows], gr(4 * is_far + k))
-        block_along_z(k)
-
     for k in range(1, 8):
-        for which in range(2):
-            net.landed(kv.at[own_rows, pl.ds(0, 128)], kr(7 * which + k - 1), when=s - k >= 0)
+        net.landed(kv.at[own_rows], kr(k - 1), when=s - k >= 0)
     for head in range(KVH):
         keys = kv[:, HD * head : HD * (head + 1)]
         values = kv[:, 128 + HD * head : 128 + HD * (head + 1)]
@@ -383,6 +389,14 @@
     for head in range(KVH):
         attend(head, GROUP - 1, 1)
 
+    of_s, of_r = net.pair(4)
+    for k in range(4):
+        part = wvo.at[:, part_of(4 * c + wrap(z - k), 128, 128)]
+        if k:
+            net.landed(part, oz_r(k - 1))
+        net.go(part, part, of_s(k), of_r(k), core_peer)
+    for k in range(4):
+        net.landed(wvo.at[:, own_lanes], of_r(k))
     attended_t = mixt[...].astype(BF16)
     attended = jnp.transpose(mixt[...]).astype(BF16)
     middle = tokens[...].astype(F32) + jnp.concatenate(
@@ -436,7 +450,7 @@
     def add_cores(off):
         exchange(off).wait()
         block = pl.ds(256 * off, 256)
-        total = own[off] + pa[1, block].astype(F32)
+        total = own[(0, 1, 0, 2)[off]] + pa[1, block].astype(F32)
         if off % 2:
             side = off // 2
             through(side).wait_recv()
@@ -490,11 +504,11 @@
             forward(0, after, nf_s, nf_r).start()
 
         pl.when(k == 1)(lambda: to_owners(0))
-        pl.when(k == 3)(lambda: to_owners(2))
+        pl.when((k == 3) & (c == 1))(lambda: to_owners(2))
 
         out_part = dot(hidden, wdv[...])
         grad_part = dot_nt(grad_gate, wgu[0]) + dot_nt(grad_up, wgu[1])
-        own[off] = jnp.where(c == 0, out_part, grad_part)
+        own[off - 2 * lax.div(off, 2) + lax.div(off, 3)] = jnp.where(c == 0, out_part, grad_part)
         pa[0, part_of(off, 256, 256)] = jnp.where(c == 0, grad_part, out_part).astype(BF16)
         exchange(off).start()
 
@@ -502,12 +516,14 @@
         forward(0, off, nf_s, nf_r).wait_send()
         forward(1, off, cf_s, cf_r).wait_send()
     net.drain()
+    pl.when(c == 0)(lambda: to_owners(2))
 
     def gradient(matrix_, store):
+        shift = y + 2 * matrix_
         for h in range(2):
             tall = dot(da[0, 448 * h : 448 * (h + 1)], gua[matrix_]).astype(BF16)
             for k in range(4):
-                store[h, wrap(k - y)] = tall[WR * k : WR * (k + 1)]
+                store[h, wrap(k - shift)] = tall[WR * k : WR * (k + 1)]
 
     gradient(0, dgate)
     zs, zr = net.pair(3)
@@ -519,8 +535,10 @@
         part = dup.at[lax.rem(xl + k, 2), pl.ds(2 * lax.div(wrap(x + k), 2), 2)]
         net.go(part, ru.at[k - 1], us(k - 1), ur(k - 1), along_x(k))
 
-    to_owners(1)
-    to_owners(3)
+    @pl.when(c == 1)
+    def _():
+        to_owners(1)
+        to_owners(3)
 
     for h in range(2):
         tall = dot(da[1, FH * h : FH * (h + 1)], acts[1]).astype(BF16)
@@ -530,6 +548,10 @@
     for q in (14, 15):
         dwd[q // 4, q % 4] = jnp.zeros((FH, 128), BF16)
 
+    zds, zdr = net.pair(3)
+    for k in range(1, 4):
+        net.go(dwd.at[:, wrap(z + k)], rzd.at[k - 1], zds(k - 1), zdr(k - 1), along_z(k))
+
     own_cot[...] = acts[1, own_tokens]
 
     @pl.loop(0, GROUP)
@@ -539,16 +561,19 @@
             scores = dot(kc[head], qs[head, :, lanes]) + mask[...]
             acts[head, :, lanes] = jnp.exp(scores - lse[GROUP * head + j, 0:1, :]).astype(BF16)
 
-    for kind in range(2):
+    def landed_parts(kind):
         for slot in range(3):
             net.landed(fr.at[kind, slot], precv(3 * kind + slot), when=None if slot else c != kind)
+        return fr[kind, 0].astype(F32) + fr[kind, 1].astype(F32) + fr[kind, 2].astype(F32)
+
+    @pl.when(c == 0)
+    def _():
+        to_owners(1)
+        to_owners(3)
+
+    grad_normed = landed_parts(1)
     middle = mid[...]
-    total = fr[0, 0].astype(F32)
-    grad_normed = fr[1, 0].astype(F32)
-    for slot in range(1, 3):
-        total = total + fr[0, slot].astype(F32)
-        grad_normed = grad_normed + fr[1, slot].astype(F32)
-    output[...] = (middle + total).astype(BF16)
+    own[0, 0:ROWS] = middle
     factor = lax.rsqrt(jnp.mean(middle * middle, axis=-1, keepdims=True) + EPS)
     unit_two = middle * factor
     scaled = grad_normed * gains[1:2, :]
@@ -586,6 +611,52 @@
     for side in range(2):
         through(side).wait_send()
 
+    def to_rows_owners(i, lanes, sems):
+        for k in range(1, 4):
+            other = part_of(xl * 4 + wrap(y + k), WR, 16)
+            net.go(
+                sa.at[i, other, lanes], rya.at[i, 0, k - 1, :, lanes], sems[0](k - 1), sems[1](k - 1),
+                place(x, wrap(y + k), z, c),
+            )
+
+    def to_rows_owners_across(i, half_size, sems):
+        for k in range(4):
+            other = part_of((1 - xl) * 4 + wrap(y + k), WR, 16)
+            for d, cut in enumerate(half_size):
+                net.go(
+                    sa.at[i, other, cut], rya.at[i, 1, k, :, cut], sems[0](3 + 2 * k + d), sems[1](3 + 2 * k + d),
+                    place(wrap(x + 1 - 2 * d), wrap(y + k), z, c),
+                )
+
+    def from_rows_owners(i, lanes, half_size, sems):
+        for k in range(1, 4):
+            net.landed(rya.at[i, 0, k - 1, :, lanes], sems[1](k - 1))
+        for k in range(4):
+            for d, cut in enumerate(half_size):
+                net.landed(rya.at[i, 1, k, :, cut], sems[1](3 + 2 * k + d))
+
+    def last_tile(i, when):
+        net.landed(xa.at[i, :, lasts_], xar(2 + i), when=when)
+
+        @pl.when(when)
+        def _():
+            sa[i, :, 384:512] = (da[i, :, last_own].astype(F32) + xa[i, :, 384:512].astype(F32)).astype(BF16)
+
+        for k in range(1, 8):
+            far = k > 3
+            other = (1 - xl if far else xl) * 4 + wrap(y + k)
+            target = place(wrap(x + (1 - 2 * i if far else 0)), wrap(y + k), z, c)
+            part = sa.at[i, part_of(other, WR, 16), lasts_]
+            net.go(part, ryl.at[i, k - 1], yl[i][0](k - 1), yl[i][1](k - 1), target, when=when)
+
+    first_cuts = ((pl.ds(0, 256), pl.ds(256, 128)), (pl.ds(0, 128), pl.ds(128, 256)))
+    yf = [net.pair(11), net.pair(11)]
+    yl = [net.pair(7), net.pair(7)]
+    net.landed(xa.at[1, :, firsts], xar(1))
+    sa[1, :, 0:384] = (da[1, :, first_own].astype(F32) + xa[1, :, 0:384].astype(F32)).astype(BF16)
+    to_rows_owners(1, firsts, yf[1])
+
+
     for k in range(1, 4):
         net.landed(ru.at[k - 1], ur(k - 1))
     for i in range(2):
@@ -605,52 +676,6 @@
     xs_s, xs_r = net.pair(3)
     for k in range(1, 4):
         net.go(sz.at[lax.rem(xl + k, 2)], rx.at[k - 1], xs_s(k - 1), xs_r(k - 1), along_x(k))
-
-    def to_rows_owners(i, lanes, half_size, sems):
-        for k in range(1, 4):
-            other = part_of(xl * 4 + wrap(y + k), WR, 16)
-            net.go(
-                sa.at[i, other, lanes], rya.at[i, 0, k - 1, :, lanes], sems[0](k - 1), sems[1](k - 1),
-                place(x, wrap(y + k), z, c),
-            )
-        for k in range(4):
-            other = part_of((1 - xl) * 4 + wrap(y + k), WR, 16)
-            for d, cut in enumerate(half_size):
-                net.go(
-                    sa.at[i, other, cut], rya.at[i, 1, k, :, cut], sems[0](3 + 2 * k + d), sems[1](3 + 2 * k + d),
-                    place(wrap(x + 1 - 2 * d), wrap(y + k), z, c),
-                )
-
-    def from_rows_owners(i, lanes, half_size, sems):
-        for k in range(1, 4):
-            net.landed(rya.at[i, 0, k - 1, :, lanes], sems[1](k - 1))
-        for k in range(4):
-            for d, cut in enumerate(half_size):
-                net.landed(rya.at[i, 1, k, :, cut], sems[1](3 + 2 * k + d))
-
-    def last_tile(i, when):
-        net.landed(xa.at[i, :, lasts_], xar(2 + i), when=when)
-
-        @pl.when(when)
-        def _():
-            sa[i, :, 384:512] = (da[i, :, last_own].astype(F32) + xa[i, :, 384:512].astype(F32)).astype(BF16)
-
-        for k in range(1, 8):
-            other, target = of_sequence(k)
-            part = sa.at[i, part_of(other, WR, 16), lasts_]
-            net.go(part, ryl.at[i, k - 1], yl[i][0](k - 1), yl[i][1](k - 1), target, when=when)
-
-    first_cuts = (pl.ds(0, 256), pl.ds(256, 128))
-    yf = [net.pair(11), net.pair(11)]
-    yl = [net.pair(7), net.pair(7)]
-    net.landed(xa.at[1, :, firsts], xar(1))
-    sa[1, :, 0:384] = (da[1, :, first_own].astype(F32) + xa[1, :, 0:384].astype(F32)).astype(BF16)
-    to_rows_owners(1, firsts, first_cuts, yf[1])
-    last_tile(1, c == 1)
-
-    zds, zdr = net.pair(3)
-    for k in range(1, 4):
-        net.go(dwd.at[:, wrap(z + k)], rzd.at[k - 1], zds(k - 1), zdr(k - 1), along_z(k))
 
     def attend_back(head, j, width):
         lanes = part_of(j, ROWS, 128) if width == 1 else pl.ds(pl.multiple_of(ROWS * j, 256), 2 * ROWS)
@@ -682,6 +707,10 @@
                 dkv.at[part_of(other, ROWS, 16), lanes], rkv.at[k - 1, :, lanes], kvs(i), kvr(i), target, when=s + k >= 8
             )
 
+    vout[...] = (own[0, 0:ROWS] + landed_parts(0)).astype(BF16)
+    out_copy = pltpu.make_async_copy(vout, out_o, lsem.at[14])
+    out_copy.start()
+
     grad_query = jnp.transpose(mixt[...]).astype(BF16)
     gqk[:, 0:384] = grad_query[:, 0:384]
     gqk[:, 512:1024] = grad_query[:, 384:D]
@@ -691,18 +720,13 @@
     net.go(da.at[0, :, first_of_peer], xa.at[0, :, firsts], xas(0), xar(0), core_peer)
     net.go(da.at[0, :, last_of_peer], xa.at[0, :, lasts_], xas(2), xar(2), core_peer, when=c == 0)
 
-    net.landed(xa.at[0, :, firsts], xar(0))
-    sa[0, :, 0:384] = (da[0, :, first_own].astype(F32) + xa[0, :, 0:384].astype(F32)).astype(BF16)
-    to_rows_owners(0, firsts, first_cuts, yf[0])
-    last_tile(0, c == 1)
-
     for k in range(1, 4):
         net.landed(rx.at[k - 1], xs_r(k - 1))
     sgu[0] = (
         sz[xl].astype(F32) + rx[0].astype(F32) + rx[1].astype(F32) + rx[2].astype(F32)
     ).astype(BF16)
     own_block = 4 * c + y
-    held = 4 * c + wrap(y - z)
+    held = [4 * c + wrap(y - z), 4 * c + wrap(y - z - 2)]
     ags, agr = net.pair(4)
     net.go(sgu.at[0], agu.at[0, own_block], ags(0), agr(0), place(x, wrap(y + z), z, c), when=z != 0)
 
@@ -730,42 +754,22 @@
     for i in range(2):
         net.go(da.at[i, :, last_of_peer], xa.at[i, :, lasts_], xas(2 + i), xar(2 + i), core_peer, when=c == 1)
 
-    for k in range(1, 4):
-        net.landed(rzd.at[k - 1], zdr(k - 1))
-    for i in range(4):
-        sdz[i] = (
-            dwd[i, z].astype(F32) + rzd[0, i].astype(F32) + rzd[1, i].astype(F32) + rzd[2, i].astype(F32)
-        ).astype(BF16)
-    xds, xdr = net.pair(3)
-    for k in range(1, 4):
-        net.go(sdz.at[wrap(x + k)], rxd.at[k - 1], xds(k - 1), xdr(k - 1), along_x(k))
-
-    owner = xh == lax.div(z, 2)
-    for k in range(4):
-        net.landed(su.at[0], vr(k), when=owner & (z != k))
-    ucs, ucr = net.pair(1)
-    uhs = net.sends(1)
-
-    @pl.when(owner)
-    def _():
-        ruz[z] = su[lax.rem(z, 2)]
-        sgu[1] = (
-            ruz[0].astype(F32) + ruz[1].astype(F32) + ruz[2].astype(F32) + ruz[3].astype(F32)
-        ).astype(BF16)
-
-    net.go(sgu.at[1], agu.at[1, own_block], ucs(0), ucr(0), place(x, wrap(y + z), z, c), when=owner & (z != 0))
-    net.go(sgu.at[1], agu.at[1, own_block], uhs(0), ucr(0), place(wrap(x + 2), wrap(y + z), z, c), when=owner)
-
-    @pl.when(owner & (z == 0))
-    def _():
-        agu[1, own_block] = sgu[1]
+    net.landed(xa.at[0, :, firsts], xar(0))
+    sa[0, :, 0:384] = (da[0, :, first_own].astype(F32) + xa[0, :, 0:384].astype(F32)).astype(BF16)
+    to_rows_owners_across(1, first_cuts[1], yf[1])
+    to_rows_owners(0, firsts, yf[0])
+    to_rows_owners_across(0, first_cuts[0], yf[0])
+    last_tile(1, c == 1)
+    last_tile(0, c == 1)
 
     grad_normed = dot_nt(gqk[...], wqk[...]) + dot_nt(grad_value, wvo[:, 384:512])
     tok = tokens[...].astype(F32)
     factor = lax.rsqrt(jnp.mean(tok * tok, axis=-1, keepdims=True) + EPS)
     unit = tok * factor
     scaled = grad_normed * gains[0:1, :]
-    gtok[...] = mid[...] + factor * (scaled - unit * jnp.mean(scaled * unit, axis=-1, keepdims=True))
+    vtok[...] = mid[...] + factor * (scaled - unit * jnp.mean(scaled * unit, axis=-1, keepdims=True))
+    tok_copy = pltpu.make_async_copy(vtok, tok_o, lsem.at[15])
+    tok_copy.start()
     gvec[0:1, :] = jnp.sum(grad_normed * unit, axis=0, keepdims=True)
     for row in range(2):
         for i in range(7):
@@ -780,28 +784,51 @@
     for k in range(1, 8):
         net.go(gsum, gy.at[k - 1], gys(k - 1), gyr(k - 1), of_sequence(k)[1])
 
-    for k in range(1, 4):
-        net.landed(rxd.at[k - 1], xdr(k - 1))
-    agd[x, z] = (
-        sdz[x].astype(F32) + rxd[0].astype(F32) + rxd[1].astype(F32) + rxd[2].astype(F32)
-    ).astype(BF16)
-    zas, zar = net.pair(3)
-    for k in range(1, 4):
-        net.go(agd.at[x, z], agd.at[x, z], zas(k - 1), zar(k - 1), along_z(k))
+    owner = xh == lax.div(z, 2)
+    for k in range(4):
+        net.landed(su.at[0], vr(k), when=owner & (z != k))
+    ucs, ucr = net.pair(1)
+    uhs = net.sends(1)
+
+    @pl.when(owner)
+    def _():
+        ruz[z] = su[lax.rem(z, 2)]
+        sgu[1] = (
+            ruz[0].astype(F32) + ruz[1].astype(F32) + ruz[2].astype(F32) + ruz[3].astype(F32)
+        ).astype(BF16)
+
+    net.go(sgu.at[1], agu.at[1, own_block], ucs(0), ucr(0), place(x, wrap(y + z + 2), z, c), when=owner & (z != 2))
+    net.go(sgu.at[1], agu.at[1, own_block], uhs(0), ucr(0), place(wrap(x + 2), wrap(y + z + 2), z, c), when=owner)
+
+    @pl.when(owner & (z == 2))
+    def _():
+        agu[1, own_block] = sgu[1]
+
+    for k in range(1, 4):
+        net.landed(rzd.at[k - 1], zdr(k - 1))
+    for i in range(4):
+        sdz[i] = (
+            dwd[i, z].astype(F32) + rzd[0, i].astype(F32) + rzd[1, i].astype(F32) + rzd[2, i].astype(F32)
+        ).astype(BF16)
+    xds, xdr = net.pair(3)
+    for k in range(1, 4):
+        net.go(sdz, rxd.at[k - 1], xds(k - 1), xdr(k - 1), along_x(k), when=lax.rem(xl + k, 2) == c)
+
 
     afs, afr = net.pair(8)
 
     def spread(matrix_, sends, recvs):
         for k in range(1, 4):
-            net.go(agu.at[matrix_, held], agu.at[matrix_, held], sends(k), recvs(k), along_z(k))
-        net.go(agu.at[matrix_, held], agu.at[matrix_, held], afs(4 * matrix_), afr(4 * matrix_), core_peer)
-
-    net.landed(agu.at[0, held], agr(0), when=z != 0)
+            net.go(agu.at[matrix_, held[matrix_]], agu.at[matrix_, held[matrix_]], sends(k), recvs(k), along_z(k))
+        part = agu.at[matrix_, held[matrix_]]
+        net.go(part, part, afs(4 * matrix_), afr(4 * matrix_), core_peer)
+
+    net.landed(agu.at[0, held[0]], agr(0), when=z != 0)
     spread(0, ags, agr)
 
     zas2, zar2 = net.pair(6)
     for i in range(2):
-        from_rows_owners(i, firsts, first_cuts, yf[i])
+        from_rows_owners(i, firsts, first_cuts[i], yf[i])
         total = sa[i, rows, 0:384].astype(F32)
         for k in range(3):
             total = total + rya[i, 0, k, :, 0:384].astype(F32)
@@ -823,15 +850,23 @@
     for k in range(1, 4):
         net.go(gz.at[3], gz.at[k - 1], zas2(k + 2), zar2(k + 2), along_z(k))
 
-    for k in range(1, 4):
-        net.landed(agd.at[x, z], zar(k - 1))
-    dxs, dxr = net.pair(3)
-    for k in range(1, 4):
-        net.go(agd.at[x], agd.at[x], dxs(k - 1), dxr(k - 1), along_x(k), when=lax.rem(xl + k, 2) == c)
-
     uas, uar = net.pair(4)
-    net.landed(agu.at[1, held], ucr(0), when=jnp.logical_not(owner) | (z != 0))
+    net.landed(agu.at[1, held[1]], ucr(0), when=jnp.logical_not(owner) | (z != 2))
     spread(1, uas, uar)
+
+    for k in range(1, 4):
+        net.landed(rxd.at[k - 1], xdr(k - 1), when=xl == c)
+    zas, zar = net.pair(3)
+
+    @pl.when(xl == c)
+    def _():
+        for i in range(4):
+            agd[i, z] = (
+                sdz[i].astype(F32) + rxd[0, i].astype(F32) + rxd[1, i].astype(F32) + rxd[2, i].astype(F32)
+            ).astype(BF16)
+
+    for k in range(1, 4):
+        net.go(agd.at[:, z], agd.at[:, z], zas(k - 1), zar(k - 1), along_z(k), when=xl == c)
 
     for k in range(1, 4):
         net.landed(rza.at[k - 1], zar2(k - 1))
@@ -861,6 +896,10 @@
         for i in range(7):
             gain_o[row : row + 1, 128 * i : 128 * (i + 1)] = gpack_sum[7 * row + i : 7 * row + i + 1]
 
+    net.drain()
+    out_copy.wait()
+    tok_copy.wait()
+
     outs = [
         pltpu.make_async_copy(aout, attn_o, lsem.at[9]),
         pltpu.make_async_copy(wide.at[0], wide_o.at[0], lsem.at[10]),
@@ -869,13 +908,13 @@
 
     def to_other_core(matrix_, recvs):
         for k in (1, 3, 2):
-            part = agu.at[matrix_, 4 * c + wrap(y - wrap(z - k))]
+            part = agu.at[matrix_, 4 * c + wrap(y - wrap(z - k) - 2 * matrix_)]
             net.landed(part, recvs(k))
             net.go(part, part, afs(4 * matrix_ + k), afr(4 * matrix_ + k), core_peer)
 
     def assemble(matrix_):
         for k in range(4):
-            net.landed(agu.at[matrix_, held], afr(4 * matrix_ + k))
+            net.landed(agu.at[matrix_, 0], afr(4 * matrix_ + k))
         for k in range(8):
             wide[matrix_, :, FC * k : FC * (k + 1)] = agu[matrix_, k]
         outs[1 + matrix_].start()
@@ -883,7 +922,7 @@
     to_other_core(0, agr)
     assemble(0)
     for k in range(1, 4):
-        net.landed(agd.at[x], dxr(k - 1), when=xl == c)
+        net.landed(agd.at[:, z], zar(k - 1), when=xl == c)
     dfs, dfr = net.pair(1)
     net.go(agd, fin, dfs(0), dfr(0), core_peer, when=xl == c)
     own_sums = pltpu.make_async_copy(agd, d_o, lsem.at[8])
@@ -909,7 +948,7 @@
 
 
 def finish_kernel(
-    out_in, tok_in, gain_in, attn_in, wide_in, down_in,
+    gain_in, out_in, tok_in, attn_in, wide_in, down_in,
     one, two, out, tok, gq, gk, gv, go, gate, up, gdown,
     vout, vtok, gain, attn, wide, down, fq, fk, fv, fo, fgate, fup, fdown, isem, osem,
 ):
@@ -988,20 +1027,21 @@
         layer_kernel,
         name="layer",
         out_shape=[
+            shape((8, D), F32),
             shape((ROWS, D), BF16),
             shape((ROWS, D), F32),
-            shape((8, D), F32),
             shape((2, WR, 1024), BF16),
             shape((2, WR, FF), BF16),
             shape((4, 4, FH, 128), BF16),
         ],
         in_specs=[vmem()] * 5 + [anywhere()] * 8,
-        out_specs=[vmem()] * 3 + [anywhere()] * 3,
+        out_specs=[vmem()] + [anywhere()] * 5,
         scratch_shapes=[
             pltpu.VMEM((8, 8, 128), F32),
             pltpu.VMEM((D, 1024), BF16),
             pltpu.VMEM((D, 1024), BF16),
-            pltpu.VMEM((8, WR, FC), BF16),
+            pltpu.VMEM((2, D, 128), BF16),
+            pltpu.VMEM((4, WR, FC), BF16),
             pltpu.VMEM((2, D, FC), BF16),
             pltpu.VMEM((FC, D), BF16),
             pltpu.VMEM((2, LENGTH, D), BF16),
@@ -1019,7 +1059,7 @@
             pltpu.VMEM((2, half, ROWS), F32),
             pltpu.VMEM((H, 8, ROWS), F32),
             pltpu.VMEM((2, LENGTH, FC), BF16),
-            pltpu.VMEM((4, 256, D), F32),
+            pltpu.VMEM((3, 256, D), F32),
             pltpu.VMEM((2, LENGTH, D), BF16),
             pltpu.VMEM((2, 3, ROWS, D), BF16),
             pltpu.VMEM((2, ROWS, D), BF16),
@@ -1042,7 +1082,7 @@
             pltpu.VMEM((2, WR, FF), BF16),
             pltpu.VMEM((3, 4, FH, 128), BF16),
             pltpu.VMEM((4, FH, 128), BF16),
-            pltpu.VMEM((3, FH, 128), BF16),
+            pltpu.VMEM((3, 4, FH, 128), BF16),
             pltpu.VMEM((4, 4, FH, 128), BF16),
             pltpu.VMEM((4, 4, FH, 128), BF16),
             pltpu.VMEM((2, D, 512), BF16),
@@ -1054,6 +1094,8 @@
             pltpu.VMEM((2, WR, 128), BF16),
             pltpu.VMEM((2, WR, 128), BF16),
             pltpu.VMEM((2, WR, 1024), BF16),
+            pltpu.VMEM((ROWS, D), BF16),
+            pltpu.VMEM((ROWS, D), F32),
             pltpu.VMEM((8, D), F32),
             pltpu.VMEM((16, 128), F32),
             pltpu.VMEM((16, 128), F32),

time: 159 us -> 156 us (0.981)
  Pallas kernels: 158 us -> 155 us
    pallas_call x1, Pallas kernels: 152 us -> 149 us  [body(): layer(tokens, segments.reshape(1, ROWS), attn_gain.reshape(1, WR), ffn_ga...]
where the time goes in v1:
time: 156 us; the launch traced here: 155 us
  Pallas kernels  155 us (99%)
    pallas_call x1, Pallas kernels, body(): layer(tokens, segments.reshape(1, ROWS), attn_gain.reshape(1, WR), ffn_ga...  149 us
    pallas_call x1, Pallas kernels, body(): one, two, out, tok, gq, gk, gv, go, gate, up, down = finish(*results)  5.6 us

profile of v1, /device:TPU:1, one launch (start us, length us, event | category | flops | bytes accessed | tf_op | source)
XLA Modules:
  0.0 155.5 jit_solution(1215481706976316680)
XLA Ops:
  0.6 149.1 %layer.1 = (f32[8,896]{1,0:T(8,128)}, bf16[128,896]{1,0:T(8,128)(2,1)}, f32[128,896]{1,0:T(8,128)}, bf16[2,112,1024]{2,1,0:T(8,128)(2,1)}, bf16[2,112,4864]{2,1,...) custom-call(bf16[128,896]{1,0:T(8,128)(2,1)} %tokens.1, s32[1,128]{1,0:T(1,128)} %bitcast.5, bf16[1,112]{1,0:T(2,128)(2,1)} %bitcast.6, ...), custom_call_target="tpu_custom_call" | custom-call | tf_op jit(solution)/shard_map/layer/pallas_call | solution.py:1114
  149.7 5.6 %finish.1 = (f32[1,112]{1,0:T(1,128)}, f32[1,112]{1,0:T(1,128)}, bf16[128,896]{1,0:T(8,128)(2,1)}, f32[128,896]{1,0:T(8,128)}, f32[112,896]{1,0:T(8,128)}, /*ind...) custom-call(f32[8,896]{1,0:T(8,128)} %get-tuple-element.28.gain_in, ...), custom_call_target="tpu_custom_call" | custom-call | tf_op jit(solution)/shard_map/finish/pallas_call | solution.py:1166

commit v2 on v1

--- a/solution.py
+++ b/solution.py
@@ -117,13 +117,13 @@
     tokens, seg, gain_one, gain_two, freq,
     cot, wq, wk, wv, wo, wg, wu, wd,
     gain_o,
-    out_o, tok_o, attn_o, wide_o, d_o,
+    vout, vtok, attn_o, wide, d_o,
     misc, wqk, wvo, wkv, st, wgu, wdv, acts, da, kv, kc, vc, kt, vt, qs, mask, mixt, mid, gains, trig, lse,
     gua, own, pa, fr, via, dgate, dup, dwd,
     gmt, own_cot, dkv, rkv, gqk,
-    rz, sz, rx, ru, su, ruz, sgu, agu, wide, rzd, sdz, rxd, agd, fin,
+    rz, sz, rx, ru, su, ruz, sgu, agu, rzd, sdz, rxd, agd, fin,
     xa, sa, rya, ryl, ta, rza, tile, rh, aout,
-    vout, vtok, gvec, gpack, gx, gsum, gy, gz, gh,
+    gvec, gpack, gx, gsum, gy, gz, gh,
     ssem, rsem, lsem,
 ):
     x, y, z, c = coords()
@@ -708,8 +708,6 @@
             )
 
     vout[...] = (own[0, 0:ROWS] + landed_parts(0)).astype(BF16)
-    out_copy = pltpu.make_async_copy(vout, out_o, lsem.at[14])
-    out_copy.start()
 
     grad_query = jnp.transpose(mixt[...]).astype(BF16)
     gqk[:, 0:384] = grad_query[:, 0:384]
@@ -768,8 +766,6 @@
     unit = tok * factor
     scaled = grad_normed * gains[0:1, :]
     vtok[...] = mid[...] + factor * (scaled - unit * jnp.mean(scaled * unit, axis=-1, keepdims=True))
-    tok_copy = pltpu.make_async_copy(vtok, tok_o, lsem.at[15])
-    tok_copy.start()
     gvec[0:1, :] = jnp.sum(grad_normed * unit, axis=0, keepdims=True)
     for row in range(2):
         for i in range(7):
@@ -897,13 +893,9 @@
             gain_o[row : row + 1, 128 * i : 128 * (i + 1)] = gpack_sum[7 * row + i : 7 * row + i + 1]
 
     net.drain()
-    out_copy.wait()
-    tok_copy.wait()
 
     outs = [
         pltpu.make_async_copy(aout, attn_o, lsem.at[9]),
-        pltpu.make_async_copy(wide.at[0], wide_o.at[0], lsem.at[10]),
-        pltpu.make_async_copy(wide.at[1], wide_o.at[1], lsem.at[11]),
     ]
 
     def to_other_core(matrix_, recvs):
@@ -917,7 +909,6 @@
             net.landed(agu.at[matrix_, 0], afr(4 * matrix_ + k))
         for k in range(8):
             wide[matrix_, :, FC * k : FC * (k + 1)] = agu[matrix_, k]
-        outs[1 + matrix_].start()
 
     to_other_core(0, agr)
     assemble(0)
@@ -948,18 +939,10 @@
 
 
 def finish_kernel(
-    gain_in, out_in, tok_in, attn_in, wide_in, down_in,
+    gain, vout, vtok, attn, wide, down,
     one, two, out, tok, gq, gk, gv, go, gate, up, gdown,
-    vout, vtok, gain, attn, wide, down, fq, fk, fv, fo, fgate, fup, fdown, isem, osem,
+    fq, fk, fv, fo, fgate, fup, fdown, osem,
 ):
-    ins = [
-        pltpu.make_async_copy(source, target, isem.at[i])
-        for i, (source, target) in enumerate(
-            [(wide_in, wide), (down_in, down), (attn_in, attn), (tok_in, vtok), (out_in, vout), (gain_in, gain)]
-        )
-    ]
-    for copy in ins:
-        copy.start()
     outs = []
 
     def store(source, target):
@@ -967,17 +950,16 @@
         copy.start()
         outs.append(copy)
 
-    ins[0].wait()
+    store(vtok, tok)
+    store(vout, out)
     fgate[...] = wide[0].astype(F32)
     store(fgate, gate)
     fup[...] = wide[1].astype(F32)
     store(fup, up)
-    ins[1].wait()
     for q in range(14):
         h, i = divmod(q, 7)
         fdown[FH * h : FH * (h + 1), 128 * i : 128 * (i + 1)] = down[q // 4, q % 4].astype(F32)
     store(fdown, gdown)
-    ins[2].wait()
     fq[:, 0:384] = attn[0, :, 0:384].astype(F32)
     fq[:, 384:D] = attn[0, :, 512:1024].astype(F32)
     store(fq, gq)
@@ -988,11 +970,6 @@
     store(fk, gk)
     fv[...] = attn[1, :, 384:512].astype(F32)
     store(fv, gv)
-    ins[3].wait()
-    store(vtok, tok)
-    ins[4].wait()
-    store(vout, out)
-    ins[5].wait()
     shard = lax.axis_index("shard")
     for k in range(8):
 
@@ -1027,15 +1004,15 @@
         layer_kernel,
         name="layer",
         out_shape=[
-            shape((8, D), F32),
-            shape((ROWS, D), BF16),
-            shape((ROWS, D), F32),
-            shape((2, WR, 1024), BF16),
-            shape((2, WR, FF), BF16),
-            shape((4, 4, FH, 128), BF16),
+            pltpu.VMEM((8, D), F32),
+            pltpu.VMEM((ROWS, D), BF16),
+            pltpu.VMEM((ROWS, D), F32),
+            pltpu.VMEM((2, WR, 1024), BF16),
+            pltpu.VMEM((2, WR, FF), BF16),
+            pltpu.VMEM((4, 4, FH, 128), BF16),
         ],
         in_specs=[vmem()] * 5 + [anywhere()] * 8,
-        out_specs=[vmem()] + [anywhere()] * 5,
+        out_specs=[vmem()] * 3 + [anywhere(), vmem(), anywhere()],
         scratch_shapes=[
             pltpu.VMEM((8, 8, 128), F32),
             pltpu.VMEM((D, 1024), BF16),
@@ -1079,7 +1056,6 @@
             pltpu.VMEM((4, WR, FC), BF16),
             pltpu.VMEM((2, WR, FC), BF16),
             pltpu.VMEM((2, 8, WR, FC), BF16),
-            pltpu.VMEM((2, WR, FF), BF16),
             pltpu.VMEM((3, 4, FH, 128), BF16),
             pltpu.VMEM((4, FH, 128), BF16),
             pltpu.VMEM((3, 4, FH, 128), BF16),
@@ -1094,8 +1070,6 @@
             pltpu.VMEM((2, WR, 128), BF16),
             pltpu.VMEM((2, WR, 128), BF16),
             pltpu.VMEM((2, WR, 1024), BF16),
-            pltpu.VMEM((ROWS, D), BF16),
-            pltpu.VMEM((ROWS, D), F32),
             pltpu.VMEM((8, D), F32),
             pltpu.VMEM((16, 128), F32),
             pltpu.VMEM((16, 128), F32),
@@ -1108,7 +1082,7 @@
             pltpu.SemaphoreType.DMA((LOCALS,)),
         ],
         compiler_params=pltpu.CompilerParams(
-            collective_id=0, has_side_effects=True, vmem_limit_bytes=60 << 20
+            collective_id=0, has_side_effects=True, vmem_limit_bytes=58 << 20
         ),
     )
     results = layer(
@@ -1142,15 +1116,9 @@
             shape((WR, FF), F32),
             shape((FC, D), F32),
         ],
-        in_specs=[anywhere()] * 6,
+        in_specs=[vmem()] * 6,
         out_specs=[vmem()] * 2 + [anywhere()] * 9,
         scratch_shapes=[
-            pltpu.VMEM((ROWS, D), BF16),
-            pltpu.VMEM((ROWS, D), F32),
-            pltpu.VMEM((8, D), F32),
-            pltpu.VMEM((2, WR, 1024), BF16),
-            pltpu.VMEM((2, WR, FF), BF16),
-            pltpu.VMEM((4, 4, FH, 128), BF16),
             pltpu.VMEM((WR, D), F32),
             pltpu.VMEM((WR, 128), F32),
             pltpu.VMEM((WR, 128), F32),
@@ -1158,10 +1126,9 @@
             pltpu.VMEM((WR, FF), F32),
             pltpu.VMEM((WR, FF), F32),
             pltpu.VMEM((FC, D), F32),
-            pltpu.SemaphoreType.DMA((6,)),
             pltpu.SemaphoreType.DMA((9,)),
         ],
-        compiler_params=pltpu.CompilerParams(vmem_limit_bytes=62 << 20),
+        compiler_params=pltpu.CompilerParams(vmem_limit_bytes=28 << 20),
     )
     one, two, out, tok, gq, gk, gv, go, gate, up, down = finish(*results)
     return out, tok, one.reshape(WR), gq, gk, gv, go, two.reshape(WR), gate, up, down

time: 156 us -> 152 us (0.974)
  Pallas kernels: 155 us -> 151 us
    pallas_call x1, Pallas kernels: 5.6 us -> 3.79 us  [body(): one, two, out, tok, gq, gk, gv, go, gate, up, down = finish(*results)]
where the time goes in v2:
time: 152 us
  Pallas kernels  151 us (99%)
    pallas_call x1, Pallas kernels, body(): layer(tokens, segments.reshape(1, ROWS), attn_gain.reshape(1, WR), ffn_ga...  148 us
    pallas_call x1, Pallas kernels, body(): one, two, out, tok, gq, gk, gv, go, gate, up, down = finish(*results)  3.79 us

profile of v2, /device:TPU:1, one launch (start us, length us, event | category | flops | bytes accessed | tf_op | source)
XLA Modules:
  0.0 152.3 jit_solution(17165263978682440588)
XLA Ops:
  0.6 147.6 %layer.1 = (f32[8,896]{1,0:T(8,128)S(1)}, bf16[128,896]{1,0:T(8,128)(2,1)S(1)}, f32[128,896]{1,0:T(8,128)S(1)}, bf16[2,112,1024]{2,1,0:T(8,128)(2,1)S(1)}, bf16[...) custom-call(bf16[128,896]{1,0:T(8,128)(2,1)} %tokens.1, s32[1,128]{1,0:T(1,128)} %bitcast.5, ...), custom_call_target="tpu_custom_call" | custom-call | tf_op jit(solution)/shard_map/layer/pallas_call | solution.py:1088
  148.3 3.8 %finish.1 = (f32[1,112]{1,0:T(1,128)}, f32[1,112]{1,0:T(1,128)}, bf16[128,896]{1,0:T(8,128)(2,1)}, f32[128,896]{1,0:T(8,128)}, f32[112,896]{1,0:T(8,128)}, /*ind...) custom-call(f32[8,896]{1,0:T(8,128)S(1)} %get-tuple-element.28.gain,, ...), custom_call_target="tpu_custom_call" | custom-call | tf_op jit(solution)/shard_map/finish/pallas_call | solution.py:1133

commit v3 on v2

--- a/solution.py
+++ b/solution.py
@@ -846,10 +846,6 @@
     for k in range(1, 4):
         net.go(gz.at[3], gz.at[k - 1], zas2(k + 2), zar2(k + 2), along_z(k))
 
-    uas, uar = net.pair(4)
-    net.landed(agu.at[1, held[1]], ucr(0), when=jnp.logical_not(owner) | (z != 2))
-    spread(1, uas, uar)
-
     for k in range(1, 4):
         net.landed(rxd.at[k - 1], xdr(k - 1), when=xl == c)
     zas, zar = net.pair(3)
@@ -863,6 +859,10 @@
 
     for k in range(1, 4):
         net.go(agd.at[:, z], agd.at[:, z], zas(k - 1), zar(k - 1), along_z(k), when=xl == c)
+
+    uas, uar = net.pair(4)
+    net.landed(agu.at[1, held[1]], ucr(0), when=jnp.logical_not(owner) | (z != 2))
+    spread(1, uas, uar)
 
     for k in range(1, 4):
         net.landed(rza.at[k - 1], zar2(k - 1))

time: 152 us -> 152 us (level)
  no operation moved by 1% of the time
where the time goes in v3:
time: 152 us
  Pallas kernels  151 us (99%)
    pallas_call x1, Pallas kernels, body(): layer(tokens, segments.reshape(1, ROWS), attn_gain.reshape(1, WR), ffn_ga...  147 us
    pallas_call x1, Pallas kernels, body(): one, two, out, tok, gq, gk, gv, go, gate, up, down = finish(*results)  3.79 us

profile of v3, /device:TPU:1, one launch (start us, length us, event | category | flops | bytes accessed | tf_op | source)
XLA Modules:
  0.0 151.6 jit_solution(17382879103043190924)
XLA Ops:
  0.6 147.0 %layer.1 = (f32[8,896]{1,0:T(8,128)S(1)}, bf16[128,896]{1,0:T(8,128)(2,1)S(1)}, f32[128,896]{1,0:T(8,128)S(1)}, bf16[2,112,1024]{2,1,0:T(8,128)(2,1)S(1)}, bf16[...) custom-call(bf16[128,896]{1,0:T(8,128)(2,1)} %tokens.1, s32[1,128]{1,0:T(1,128)} %bitcast.5, ...), custom_call_target="tpu_custom_call" | custom-call | tf_op jit(solution)/shard_map/layer/pallas_call | solution.py:1088
  147.7 3.8 %finish.1 = (f32[1,112]{1,0:T(1,128)}, f32[1,112]{1,0:T(1,128)}, bf16[128,896]{1,0:T(8,128)(2,1)}, f32[128,896]{1,0:T(8,128)}, f32[112,896]{1,0:T(8,128)}, /*ind...) custom-call(f32[8,896]{1,0:T(8,128)S(1)} %get-tuple-element.28.gain,, ...), custom_call_target="tpu_custom_call" | custom-call | tf_op jit(solution)/shard_map/finish/pallas_call | solution.py:1133
